TPU v7x, 128 devices: a whole 4x4x4 slice. The times are simulated.
128 devices in a mesh: dp: 128 (over x, y, z, core).
Axes of the slice: x: 4, y: 4, z: 4, core: 2. Of those that a mesh axis runs over, the one named last changes fastest.
Arguments:
- grad_query: bfloat16 [128, 64, 8192], P('dp'), may hold values from -6 to 6
- grad_gate: bfloat16 [128, 128, 8192], P('dp'), may hold values from -24 to 24
- old_master: float32 [2883584], P('dp'), may hold values from -6 to 6
- old_moment: float32 [2883584], P('dp'), may hold values from -6 to 6
- old_variance: float32 [2883584], P('dp'), may hold values from 0.5 to 8
- old_bounds: int32 [128, 2], P('dp'), may hold values from 0 to 1572864, as said below
Outputs:
- new_master: float32 [1572864], P('dp')
- new_moment: float32 [1572864], P('dp')
- new_variance: float32 [1572864], P('dp')
- query_weight: bfloat16 [64, 8192], replicated
- gate_weight: bfloat16 [128, 8192], replicated
Inputs may be any that keep to these rules, and one draw needn't show every extreme that they name: `old_bounds`: the 96 old buckets, in the order of old owners, tile 0 to 1572864: old owner i's bucket stands in row 4 (i // 3) + i % 3, and the last ends at 1572864. Old owner 3k starts exactly at 4 k * 12288; every other start lies on a multiple of 128 within 3072 of i * 16384. A row whose index is 3 mod 4 holds an empty bucket, both entries equal to the end of the row before it. One bucket has exactly 22528 positions.
All inputs are finite; a program needn't handle non-finite values.
Results may differ from a plain program's by a relative error of at most 0.001.
Values may be sent and summed in bfloat16 or wider, within the bound.
A program may use at most 64 MiB of HBM per device.

v0:
```python
import jax
import jax.numpy as jnp
from jax import lax
from jax.sharding import PartitionSpec as P

STEP = 10


beta_one = 0.9
beta_two = 0.95
learn_rate = 0.01
decay_rate = 0.1
epsilon = 1e-08


def shifted(array, axis, by):
    length = lax.axis_size(axis)
    pairs = [(i, i + by) for i in range(length) if 0 <= i + by < length]
    return lax.ppermute(array, axis, pairs)


def adamw_step(master, moment, variance, grad):
    moment_new = beta_one * moment + (1.0 - beta_one) * grad
    variance_new = beta_two * variance + (1.0 - beta_two) * grad * grad
    corrected_m = moment_new / (1.0 - beta_one**STEP)
    corrected_v = variance_new / (1.0 - beta_two**STEP)
    master_new = master - learn_rate * (
        corrected_m / (jnp.sqrt(corrected_v) + epsilon) + decay_rate * master
    )
    return (master_new, moment_new, variance_new)


def on_device(grad_query, grad_gate, old_master, old_moment, old_variance, old_bounds):
    owners = lax.axis_size("dp")
    device_index = lax.axis_index("dp")
    query_rows = grad_query.shape[1]
    row_width = grad_query.shape[2]
    flat_count = (query_rows + grad_gate.shape[1]) * row_width
    shard_len = flat_count // owners
    bucket_start = old_bounds[0, 0]
    finish = old_bounds[0, 1]
    shard_base = device_index * shard_len
    stacked = jnp.stack([old_master, old_moment, old_variance])
    padded = jnp.pad(stacked, ((0, 0), (2 * shard_len, 2 * shard_len)))

    def window(first):
        offset = first - bucket_start + 2 * shard_len
        piece_data = lax.dynamic_slice_in_dim(padded, offset, shard_len, 1)
        where_at = first + jnp.arange(shard_len, dtype=jnp.int32)
        inside = (where_at >= bucket_start) & (where_at < finish)
        return jnp.where(inside[None, :], piece_data, 0.0)

    own_part = window(shard_base)
    after_part = window(shard_base + shard_len)
    from_before = shifted(after_part, "dp", 1)
    arrived = own_part + from_before
    flat_local = jnp.concatenate([grad_query.reshape(-1), grad_gate.reshape(-1)])
    grad_shard = lax.psum_scatter(
        flat_local.astype(jnp.float32), "dp", scatter_dimension=0, tiled=True
    )
    master_new, moment_new, variance_new = adamw_step(
        arrived[0], arrived[1], arrived[2], grad_shard
    )
    gathered = lax.all_gather(master_new.astype(jnp.bfloat16), "dp", axis=0, tiled=True)
    query_weight = gathered[: query_rows * row_width].reshape(query_rows, row_width)
    gate_weight = gathered[query_rows * row_width :].reshape(-1, row_width)
    return (master_new, moment_new, variance_new, query_weight, gate_weight)


def solution(mesh):
    placed = (P("dp", None, None), P("dp", None, None), P("dp"), P("dp"), P("dp"), P("dp", None))
    return jax.shard_map(
        on_device,
        mesh=mesh,
        in_specs=placed,
        out_specs=(P("dp"), P("dp"), P("dp"), P(), P()),
        check_vma=False,
    )
```

profile of v0, /device:TPU:1, one launch (start us, length us, event | category | flops | bytes accessed | tf_op | source)
XLA Modules:
  0.0 269.8 jit_solution(6404809373391803164)
XLA Ops:
  7.2 0.0 all-reduce.4.cloned.1.call-start
  7.2 1.3 fusion.10
  9.2 1.3 fusion.7
  10.5 1.3 select_maximum_fusion
  11.8 0.2 dynamic-slice_select_fusion
  12.0 4.9 %collective-permute-start = (f32[3,12288]{1,0:T(4,128)S(1)}, f32[3,12288]{1,0:T(4,128)S(1)}, u32[]{:S(2)}, u32[]{:S(2)}) collective-permute-start(f32[3,12288]{1,0:T(4,128)S(1)} %dynamic-slice_select_fusion), channel_id=1, source_target_pairs={{0,1},{1,2},{2,3},{3,4},{4,5},{5,6},{6,7},{7,8},{8,9},{9,10},{10,1... | collective-permute-start | bytes 442376 | tf_op jit(solution)/shard_map/ppermute | solution.py:19
  16.9 0.0 copy-start
  17.0 2.3 copy.12
  19.2 0.0 copy-done
  19.2 0.3 copy.11
  19.5 9.0 %maximum_convert_fusion = f32[1572864]{0:T(1024)} fusion(bf16[1048576]{0:T(1024)(128)(2,1)S(1)} %bitcast.12, bf16[524288]{0:T(1024)(128)(2,1)S(1)} %bitcast.13), kind=kLoop, calls=%fused_computation | loop fusion | flops 6291456 | bytes 9437184 | tf_op jit(solution)/shard_map/convert_element_type | solution.py:59
  28.5 0.0 all-reduce.4.cloned.1.call-update
  28.5 0.0 all-gather.2.cloned.1.call-start
  29.2 1.3 fusion.6
  30.5 0.0 collective-permute-done
  30.5 0.2 select_add_fusion
  30.7 0.1 slice_multiply_fusion
  30.9 157.4 %all-reduce.4.cloned.1.call-done = f32[1572864]{0:T(1024)} async-done(((f32[1572864]{0:T(1024)}), f32[1572864]{0:T(1024)}) %all-reduce.4.cloned.1.call-update) | async-done | bytes 6291472
  188.3 1.5 fusion.8
  189.8 0.0 all-gather.2.cloned.1.call-update
  189.8 66.8 %all-gather.2.cloned.1.call-done = bf16[1572864]{0:T(1024)(128)(2,1)} async-done(((bf16[12288]{0:T(1024)(128)(2,1)}), bf16[1572864]{0:T(1024)(128)(2,1)}) %all-gather.2.cloned.1.call-update) | async-done | bytes 3145744 | tf_op jit(solution)/shard_map/all_gather | solution.py:64
  256.6 0.0 slice-start
  256.6 1.6 slice-done
  258.2 2.3 slice.49
  260.4 0.0 slice-start.1
  260.4 1.2 slice-done.1
  261.7 1.3 slice.47
Async XLA Ops:
  7.2 181.1 %all-reduce.4.cloned.1.call-start = ((), (), s32[]{:S(2)}) async-start(), calls=%async_computation.1 | async-start | bytes 12582912
  12.0 18.5 %collective-permute-start = (f32[3,12288]{1,0:T(4,128)S(1)}, f32[3,12288]{1,0:T(4,128)S(1)}, u32[]{:S(2)}, u32[]{:S(2)}) collective-permute-start(f32[3,12288]{1,0:T(4,128)S(1)} %dynamic-slice_select_fusion), channel_id=1, source_target_pairs={{0,1},{1,2},{2,3},{3,4},{4,5},{5,6},{6,7},{7,8},{8,9},{9,10},{10,1... | collective-permute-start | bytes 442376 | tf_op jit(solution)/shard_map/ppermute | solution.py:19
  16.9 2.3 copy-start
  28.5 228.1 %all-gather.2.cloned.1.call-start = ((), (), s32[]{:S(2)}) async-start(), calls=%async_computation | async-start | bytes 3170304 | tf_op jit(solution)/shard_map/all_gather | solution.py:64
  256.6 1.6 slice-start
  260.4 1.2 slice-start.1
Sparse Core Ops, SparseCore 0:
  28.6 159.6 all-reduce.3
  191.9 64.6 all-gather.1
where the time goes:
time: 270 us
  waiting for transfers between devices  224 us (83%)
  between operations  15.5 us (6%)
  other arithmetic  14.9 us (6%)
  local copies, waits for them, and re-layouts  10.2 us (4%)
  starting transfers between devices  5.02 us (2%)
    unnamed x3, waiting for transfers between devices  157 us
    all_gather x1, waiting for transfers between devices, on_device(): lax.all_gather(master_new.astype(jnp.bfloat16), 'dp', axis=0, tiled=True)  66.8 us
    convert_element_type x1, other arithmetic, on_device(): flat_local.astype(jnp.float32)  8.97 us
  transfers between devices with their start and end apart: 3, of which 2 were waited for; matrix products, arithmetic and copies ran while one was open for 5% of the time, Pallas kernels for 0%

commit v1 on v0

v1 whole, which is shorter than its diff:
```python
import functools

import jax
import jax.numpy as jnp
from jax import lax
from jax.experimental import pallas as pl
from jax.experimental.pallas import tpu as pltpu
from jax.sharding import PartitionSpec as P

MESH = pl.DeviceIdType.MESH
F32 = jnp.float32
BF16 = jnp.bfloat16

STEP = 10
beta_one = 0.9
beta_two = 0.95
learn_rate = 0.01
decay_rate = 0.1
epsilon = 1e-08

LANE = 128
BLK = 32
ORDER = ((0, 1, 2), (1, 2, 0), (2, 0, 1))


def adamw_step(master, moment, variance, grad):
    moment_new = beta_one * moment + (1.0 - beta_one) * grad
    variance_new = beta_two * variance + (1.0 - beta_two) * grad * grad
    corrected_m = moment_new / (1.0 - beta_one**STEP)
    corrected_v = variance_new / (1.0 - beta_two**STEP)
    master_new = master - learn_rate * (
        corrected_m / (jnp.sqrt(corrected_v) + epsilon) + decay_rate * master
    )
    return (master_new, moment_new, variance_new)


def kernel(
    stop,
    query, gate, old_m, old_v, old_s, bounds,
    new_m, new_v, new_s, weights,
    mine, other, s0, r1, s1, r2, s2, r3, state, passed, arrived,
    load_sem, s0_send, s0_recv, s1_send, s1_recv, s2_send, s2_recv, s3_send, s3_recv,
    x_send, x_recv, g_send, g_recv, c_send, c_recv, p_send, p_recv,
):
    me = lax.axis_index("dp")
    core = me % 2
    chip = me // 2
    at = (chip // 16, (chip // 4) % 4, chip % 4)
    sibling = me + 1 - 2 * core

    def device(axis, by, on_core):
        place = list(at)
        place[axis] = (place[axis] + by) % 4
        return ((place[0] * 4 + place[1]) * 4 + place[2]) * 2 + on_core

    def remote(src, dst, send, recv, to):
        return pltpu.make_async_remote_copy(
            src_ref=src, dst_ref=dst, send_sem=send, recv_sem=recv,
            device_id=(to,), device_id_type=MESH,
        )

    sent = []

    loads = [
        pltpu.make_async_copy(query.at[:, core], mine.at[pl.ds(0, 64)], load_sem.at[0]),
        pltpu.make_async_copy(gate.at[:, core], mine.at[pl.ds(64, 128)], load_sem.at[1]),
    ]
    for n, old in enumerate((old_m, old_v, old_s)):
        loads.append(
            pltpu.make_async_copy(old, state.at[n, pl.ds(96, 176)], load_sem.at[2 + n])
        )
    for copy in loads:
        copy.start()

    barrier = pltpu.get_barrier_semaphore()

    def greet(to):
        pl.semaphore_signal(barrier, inc=1, device_id=(to,), device_id_type=MESH)

    greet(sibling)
    for axis in range(3):
        for by in (1, 2, 3):
            greet(device(axis, by, core))

    @pl.when(core == 0)
    def _():
        for by in (1, 2, 3):
            greet(device(2, by, 1))

    @pl.when(core == 1)
    def _():
        for by in (1, 2, 3):
            greet(device(1, by, 0))

    pl.semaphore_wait(barrier, 13)

    swaps = [
        remote(query.at[:, 1 - core], other.at[pl.ds(0, 64)], s0_send.at[0], s0_recv.at[0], sibling),
        remote(gate.at[:, 1 - core], other.at[pl.ds(64, 128)], s0_send.at[1], s0_recv.at[1], sibling),
    ]
    for copy in swaps:
        copy.start()
    sent += swaps

    for n in range(3):
        state[n, pl.ds(0, 96)] = jnp.zeros((96, LANE), F32)
        state[n, pl.ds(272, 96)] = jnp.zeros((96, LANE), F32)
    for copy in loads[2:]:
        copy.wait()
    first = bounds[0, 0] // LANE
    last = bounds[0, 1] // LANE

    def window(n, base):
        rows = lax.broadcasted_iota(jnp.int32, (96, LANE), 0) + base
        piece = state[n, pl.ds(jnp.clip(base - first + 96, 0, 272), 96)]
        return jnp.where((rows >= first) & (rows < last), piece, 0.0)

    for n in range(3):
        passed[n] = window(n, (me + 1) * 96)
    hands_on = (core == 0) | (at[2] % 2 == 0)
    takes = (core == 1) | (at[2] % 2 == 1)
    handed = remote(
        passed, arrived, p_send.at[0], p_recv.at[0],
        sibling * (1 - core) + device(2, 1, 0) * core,
    )

    @pl.when(hands_on)
    def _():
        handed.start()

    for copy in loads[:2]:
        copy.wait()
    for copy in swaps:
        copy.wait_recv()

    def pair(i, carry):
        i_x, i_y = i // 4, i % 4
        for z in range(4):
            to = (4 * i + z, i_y * 16 + z * 4 + i_x, z * 16 + i_x * 4 + i_y)
            for p in range(3):
                row = 12 * i + 3 * z + p
                s0[p, to[p]] = mine[row].astype(F32) + other[row].astype(F32)
        return carry

    lax.fori_loop(0, 16, pair, 0)
    if stop == 0:
        return finish(stop, sent, handed, hands_on, takes, new_m, new_v, new_s, weights, s0)

    copies1 = {}
    for by in (2, 1, 3):
        for p in range(3):
            a = ORDER[p][0]
            copies1[p, by] = remote(
                s0.at[p, pl.ds((at[a] + by) % 4 * 16, 16)], r1.at[p, by - 1],
                s1_send.at[p * 3 + by - 1], s1_recv.at[p * 3 + by - 1], device(a, by, core),
            )
            copies1[p, by].start()
            sent.append(copies1[p, by])
    copies2 = {}
    for p in range(3):
        a, b, _ = ORDER[p]
        for by in (1, 2, 3):
            copies1[p, by].wait_recv()
        own = at[a] * 16

        def second(i, carry, p=p, own=own):
            s1[p, i] = (s0[p, own + i] + r1[p, 0, i]) + (r1[p, 1, i] + r1[p, 2, i])
            return carry

        lax.fori_loop(0, 16, second, 0)
        if stop == 1:
            continue
        for by in (2, 1, 3):
            copies2[p, by] = remote(
                s1.at[p, pl.ds((at[b] + by) % 4 * 4, 4)], r2.at[p, by - 1],
                s2_send.at[p * 3 + by - 1], s2_recv.at[p * 3 + by - 1], device(b, by, core),
            )
            copies2[p, by].start()
            sent.append(copies2[p, by])
    if stop == 1:
        return finish(stop, sent, handed, hands_on, takes, new_m, new_v, new_s, weights, s0)

    for p in range(3):
        _, b, c = ORDER[p]
        for by in (1, 2, 3):
            copies2[p, by].wait_recv()
        for i in range(4):
            own = at[b] * 4 + i
            s2[p, i] = (s1[p, own] + r2[p, 0, i]) + (r2[p, 1, i] + r2[p, 2, i])
        if stop == 2:
            continue
        unit = 2 * p + core
        owner = unit // 3
        place = unit % 3
        for by in (2, 1, 3):
            copy = remote(
                s2.at[p, (at[c] + by) % 4], r3.at[place, at[c]],
                s3_send.at[p * 4 + by], s3_recv.at[place * 4 + at[c]], device(c, by, owner),
            )
            copy.start()
            sent.append(copy)

        if p != 1:
            local = remote(
                s2.at[p, at[c]], r3.at[place, at[c]],
                s3_send.at[p * 4], s3_recv.at[place * 4 + at[c]], sibling,
            )
            crosses = core == (1 if p == 0 else 0)

            @pl.when(crosses)
            def _(local=local):
                local.start()
                local.wait_send()

            @pl.when(jnp.logical_not(crosses))
            def _(p=p, place=place, c=c):
                r3[place, at[c]] = s2[p, at[c]]
        else:
            r3[place, at[c]] = s2[p, at[c]]
    if stop == 2:
        return finish(stop, sent, handed, hands_on, takes, new_m, new_v, new_s, weights, s0)

    @pl.when(takes)
    def _():
        handed.wait_recv()

    @pl.when(jnp.logical_not(takes))
    def _():
        arrived[...] = jnp.zeros_like(arrived)

    own_state = [window(n, me * 96) + arrived[n] for n in range(3)]
    for n, ref in enumerate((new_m, new_v, new_s)):
        ref[...] = own_state[n]

    last_at = (
        at[2] * (1 - core) + at[0] * core,
        at[2] * (1 - core) + at[1] * core,
        at[0] * (1 - core) + at[1] * core,
    )
    gathers = {}
    for m in range(3):
        for by in range(4):
            if by == 0 and m != 1:
                continue
            src = (last_at[m] + by) % 4
            remote(
                r3.at[m, src], r3.at[m, src], s3_send.at[0], s3_recv.at[m * 4 + src], sibling
            ).wait_recv()
        rows = pl.ds(m * BLK, BLK)
        grad = (r3[m, 0] + r3[m, 1]) + (r3[m, 2] + r3[m, 3])
        master, moment, variance = adamw_step(new_m[rows], new_v[rows], new_s[rows], grad)
        new_m[rows] = master
        new_v[rows] = moment
        new_s[rows] = variance
        weights[at[0], at[1], at[2], 3 * core + m] = master.astype(BF16)
        if stop == 3:
            continue
        c = ORDER[m][2]
        block = weights.at[at[0], at[1], at[2], 3 * core + m]
        for by in (2, 1, 3):
            gathers[m, by] = remote(
                block, block, g_send.at[m * 3 + by - 1], g_recv.at[m * 3 + by - 1], device(c, by, core)
            )
            gathers[m, by].start()
            sent.append(gathers[m, by])
    if stop == 3:
        return finish(stop, sent, handed, hands_on, takes, new_m, new_v, new_s, weights, s0)

    def slab(m, free, where):
        index = [slice(None) if axis in free else where[axis] for axis in range(3)]
        return weights.at[index[0], index[1], index[2], 3 * core + m]

    def moved(axis, by):
        place = list(at)
        place[axis] = (place[axis] - by) % 4
        return place

    def await_slab(m, free, axis, by, sem):
        src = slab(m, free, moved(axis, by))
        remote(src, src, g_send.at[0], sem, sibling).wait_recv()

    for level in (1, 2):
        for m in range(3):
            a, b, c = ORDER[m]
            before, axis = ((c, b) if level == 1 else (b, a))
            held = () if level == 1 else (c,)
            for by in (1, 2, 3):
                await_slab(m, held, before, by, g_recv.at[(level - 1) * 9 + m * 3 + by - 1])
            free = held + (before,)
            block = slab(m, free, at)
            for by in (2, 1, 3):
                number = level * 9 + m * 3 + by - 1
                copy = remote(
                    block, block, g_send.at[number], g_recv.at[number], device(axis, by, core)
                )
                copy.start()
                sent.append(copy)
            if level == 2:
                copy = remote(block, block, c_send.at[m * 4], c_recv.at[m * 4], sibling)
                copy.start()
                sent.append(copy)
    if stop == 4:
        for m in range(3):
            a, b, c = ORDER[m]
            for by in (1, 2, 3):
                await_slab(m, (b, c), a, by, g_recv.at[18 + m * 3 + by - 1])
            src = slab(m, (b, c), at)
            remote(src, src, c_send.at[0], c_recv.at[m * 4], sibling).wait_recv()
        return finish(stop, sent, handed, hands_on, takes, new_m, new_v, new_s, weights, s0)
    for by in (1, 3, 2):
        for m in range(3):
            a, b, c = ORDER[m]
            await_slab(m, (b, c), a, by, g_recv.at[18 + m * 3 + by - 1])
            block = slab(m, (b, c), moved(a, by))
            copy = remote(block, block, c_send.at[m * 4 + by], c_recv.at[m * 4 + by], sibling)
            copy.start()
            sent.append(copy)
    for m in range(3):
        a, b, c = ORDER[m]
        for by in range(4):
            index = moved(a, by)
            index = [slice(None) if axis in (b, c) else index[axis] for axis in range(3)]
            src = weights.at[index[0], index[1], index[2], 3 * (1 - core) + m]
            remote(src, src, c_send.at[0], c_recv.at[m * 4 + by], sibling).wait_recv()
    finish(stop, sent, handed, hands_on, takes, None, None, None, None, None)


def finish(stop, sent, handed, hands_on, takes, new_m, new_v, new_s, weights, s0):
    for copy in sent:
        copy.wait_send()

    @pl.when(hands_on)
    def _():
        handed.wait_send()

    if stop < 3:
        @pl.when(takes)
        def _():
            handed.wait_recv()
        for ref in (new_m, new_v, new_s):
            ref[...] = jnp.zeros_like(ref)
        weights[0, 0, 0, 0] = s0[0, 0].astype(BF16)


def on_device(grad_query, grad_gate, old_master, old_moment, old_variance, old_bounds, stop=9):
    query_rows, row_width = grad_query.shape[1:]
    gate_rows = grad_gate.shape[1]
    query = grad_query.reshape(query_rows, 2, BLK, LANE)
    gate = grad_gate.reshape(gate_rows, 2, BLK, LANE)
    old = [a.reshape(-1, LANE) for a in (old_master, old_moment, old_variance)]
    any_space = pl.BlockSpec(memory_space=pl.ANY)
    vmem = pl.BlockSpec(memory_space=pltpu.VMEM)
    dma = pltpu.SemaphoreType.DMA
    shard = jax.ShapeDtypeStruct((96, LANE), F32)
    new_m, new_v, new_s, weights = pl.pallas_call(
        functools.partial(kernel, stop),
        out_shape=(shard, shard, shard, jax.ShapeDtypeStruct((4, 4, 4, 6, BLK, LANE), BF16)),
        in_specs=[any_space] * 5 + [pl.BlockSpec(memory_space=pltpu.SMEM)],
        out_specs=(vmem, vmem, vmem, vmem),
        scratch_shapes=[
            pltpu.VMEM((192, BLK, LANE), BF16),
            pltpu.VMEM((192, BLK, LANE), BF16),
            pltpu.VMEM((3, 64, BLK, LANE), F32),
            pltpu.VMEM((3, 3, 16, BLK, LANE), F32),
            pltpu.VMEM((3, 16, BLK, LANE), F32),
            pltpu.VMEM((3, 3, 4, BLK, LANE), F32),
            pltpu.VMEM((3, 4, BLK, LANE), F32),
            pltpu.VMEM((3, 4, BLK, LANE), F32),
            pltpu.VMEM((3, 368, LANE), F32),
            pltpu.VMEM((3, 96, LANE), F32),
            pltpu.VMEM((3, 96, LANE), F32),
            dma((5,)),
            dma((2,)), dma((2,)),
            dma((9,)), dma((9,)),
            dma((9,)), dma((9,)),
            dma((12,)), dma((12,)),
            dma((1,)), dma((1,)),
            dma((27,)), dma((27,)),
            dma((12,)), dma((12,)),
            dma((1,)), dma((1,)),
        ],
        compiler_params=pltpu.CompilerParams(
            collective_id=0, has_side_effects=True, vmem_limit_bytes=40 * 1024 * 1024
        ),
    )(query, gate, *old, old_bounds)
    flat = weights.reshape(-1)
    split = query_rows * row_width
    return (
        new_m.reshape(-1), new_v.reshape(-1), new_s.reshape(-1),
        flat[:split].reshape(query_rows, row_width),
        flat[split:].reshape(gate_rows, row_width),
    )


def solution(mesh, stop=9):
    placed = (P("dp", None, None), P("dp", None, None), P("dp"), P("dp"), P("dp"), P("dp", None))
    return jax.shard_map(
        functools.partial(on_device, stop=stop),
        mesh=mesh,
        in_specs=placed,
        out_specs=(P("dp"), P("dp"), P("dp"), P(), P()),
        check_vma=False,
    )
```

time: 270 us -> 68 us (0.25)
  waiting for transfers between devices: 224 us -> 0 us
  Pallas kernels: 0 us -> 53.7 us
  other arithmetic: 14.9 us -> 0 us
  between operations: 15.5 us -> 0.67 us
  starting transfers between devices: 5.02 us -> 0 us
  local copies, waits for them, and re-layouts: 10.2 us -> 13.4 us
    unnamed x3 -> x0, waiting for transfers between devices: 157 us -> none
    all_gather x1 -> x0, waiting for transfers between devices: 66.8 us -> none  [on_device(): lax.all_gather(master_new.astype(jnp.bfloat16), 'dp', axis=0, tiled=True)]
    pallas_call x0 -> x1, Pallas kernels: none -> 53.7 us  [on_device(): pl.pallas_call(functools.partial(kernel, stop), out_shape=(shard, shard,...]
    convert_element_type x2 -> x0, other arithmetic: 10.4 us -> none  [the longest x1 8.97 us: on_device(): flat_local.astype(jnp.float32)]
    ppermute x1 -> x0, starting transfers between devices: 4.94 us -> none  [shifted(): return lax.ppermute(array, axis, pairs)]
    slice x7 -> x3, local copies, waits for them, and re-layouts: 7.66 us -> 8.68 us  [the longest x2 5.58 us: on_device(): flat[:split].reshape(query_rows, row_width)]
  transfers between devices with their start and end apart: 3 -> 0, of which waited for: 2 -> 0; matrix products, arithmetic and copies ran while one was open for 5% -> 0% of each run, Pallas kernels for 0% -> 0%
where the time goes in v1:
time: 68 us; the launch traced here: 67.7 us
  Pallas kernels  53.7 us (79%)
  local copies, waits for them, and re-layouts  13.4 us (20%)
    pallas_call x1, Pallas kernels, on_device(): pl.pallas_call(functools.partial(kernel, stop), out_shape=(shard, shard,...  53.7 us
    slice x2, local copies, waits for them, and re-layouts, on_device(): flat[:split].reshape(query_rows, row_width)  5.58 us
    unnamed x15, local copies, waits for them, and re-layouts  4.73 us
    slice x1, local copies, waits for them, and re-layouts, on_device(): flat[split:].reshape(gate_rows, row_width)  3.09 us

profile of v1, /device:TPU:1, one launch (start us, length us, event | category | flops | bytes accessed | tf_op | source)
XLA Modules:
  0.0 67.7 jit_solution(16290885187210815606)
XLA Ops:
  0.6 0.0 copy-start.4
  0.6 1.6 %copy.11 = bf16[8,8,64,128]{3,2,1,0:T(8,128)(2,1)S(1)} copy(bf16[8,8,64,128]{3,1,2,0:T(8,128)(2,1)} %bitcast.25) | data formatting | bytes 2097152
  2.3 0.2 copy-done.4
  2.5 0.0 copy-start
  2.5 0.0 copy-start.1
  2.5 0.0 copy-start.2
  2.5 0.0 copy-start.3
  2.5 0.6 copy.12
  3.2 0.3 copy-done
  3.4 0.0 copy-done.1
  3.5 0.0 copy-done.2
  3.5 0.0 copy-done.3
  3.5 53.7 %shard_map.101 = (f32[96,128]{1,0:T(8,128)S(1)}, f32[96,128]{1,0:T(8,128)S(1)}, f32[96,128]{1,0:T(8,128)S(1)}, bf16[4,4,4,6,32,128]{5,4,3,2,1,0:T(8,128)(2,1)S(1)}) custom-call(bf16[64,2,32,128]{3,2,1,0:T(8,128)(2,1)S(1)} %bitcast.17, bf16[128,2,32,128]{3,2,1,0:T(8,128)(2,1)S(1)} %bitcast.16, f32[176,128]{1,0:T(8,128)S(1)} %bitcast.18, ...), custom_call_target="tpu_custom_call" | custom-call | tf_op jit(solution)/shard_map/pallas_call | solution.py:355
  57.2 3.3 %slice.10 = bf16[192,8192]{1,0:T(8,128)(2,1)} reshape(bf16[4,4,4,6,32,128]{5,4,3,2,1,0:T(8,128)(2,1)S(1)} %get-tuple-element.12) | data formatting | bytes 6291456 | tf_op jit(solution)/shard_map/slice | solution.py:390
  60.5 2.3 %slice.13 = bf16[64,8192]{1,0:T(8,128)(2,1)} slice(bf16[192,8192]{1,0:T(8,128)(2,1)} %slice.10), slice={[0:64], [0:8192]} | slice | bytes 2097152 | tf_op jit(solution)/shard_map/slice | solution.py:390
  62.8 3.1 %slice.14 = bf16[128,8192]{1,0:T(8,128)(2,1)} slice(bf16[192,8192]{1,0:T(8,128)(2,1)} %slice.10), slice={[64:192], [0:8192]} | slice | bytes 4194304 | tf_op jit(solution)/shard_map/slice | solution.py:391
  65.9 0.6 copy.16
  66.5 0.6 copy.17
  67.1 0.6 copy.18
Async XLA Ops:
  0.6 1.9 %copy-start.4 = (bf16[1,128,8192]{2,1,0:T(8,128)(2,1)S(1)}, bf16[1,128,8192]{2,1,0:T(8,128)(2,1)}, u32[]{:S(2)}) copy-start(bf16[1,128,8192]{2,1,0:T(8,128)(2,1)} %param.7) | copy-start | bytes 6291460
  2.5 0.9 %copy-start = (f32[22528]{0:T(1024)S(1)}, f32[22528]{0:T(1024)}, u32[]{:S(2)}) copy-start(f32[22528]{0:T(1024)} %param.8) | copy-start | bytes 270340
  2.5 0.9 %copy-start.1 = (f32[22528]{0:T(1024)S(1)}, f32[22528]{0:T(1024)}, u32[]{:S(2)}) copy-start(f32[22528]{0:T(1024)} %param.9) | copy-start | bytes 270340
  2.5 1.0 %copy-start.2 = (f32[22528]{0:T(1024)S(1)}, f32[22528]{0:T(1024)}, u32[]{:S(2)}) copy-start(f32[22528]{0:T(1024)} %param.10) | copy-start | bytes 270340
  2.5 1.0 %copy-start.3 = (s32[1,2]{1,0:T(1,128)S(1)}, s32[1,2]{1,0:T(1,128)}, u32[]{:S(2)}) copy-start(s32[1,2]{1,0:T(1,128)} %bounds.1) | copy-start | bytes 28

commit v2 on v1

--- a/solution.py
+++ b/solution.py
@@ -19,6 +19,7 @@
 epsilon = 1e-08
 
 LANE = 128
+PITCH = 40
 BLK = 32
 ORDER = ((0, 1, 2), (1, 2, 0), (2, 0, 1))
 
@@ -61,15 +62,23 @@
 
     sent = []
 
-    loads = [
-        pltpu.make_async_copy(query.at[:, core], mine.at[pl.ds(0, 64)], load_sem.at[0]),
-        pltpu.make_async_copy(gate.at[:, core], mine.at[pl.ds(64, 128)], load_sem.at[1]),
-    ]
+    half = mine.shape[1]
+    pieces = ((query, 0, 0, 48), (query, 48, 48, 16), (gate, 0, 64, 32), (gate, 32, 96, 48), (gate, 80, 144, 48))
+    of_chunk = ((0,), (1, 2), (3,), (4,))
+    own_half = pl.ds(pl.multiple_of(core * half, half), half)
+    its_half = pl.ds(pl.multiple_of((1 - core) * half, half), half)
+    loads, olds, swaps = [], [], []
+    for n, (array, start, row, rows) in enumerate(pieces):
+        loads.append(pltpu.make_async_copy(
+            array.at[pl.ds(start, rows), own_half], mine.at[pl.ds(row, rows)], load_sem.at[n]))
+        swaps.append(remote(
+            array.at[pl.ds(start, rows), its_half], other.at[pl.ds(row, rows)],
+            s0_send.at[n], s0_recv.at[n], sibling))
     for n, old in enumerate((old_m, old_v, old_s)):
-        loads.append(
-            pltpu.make_async_copy(old, state.at[n, pl.ds(96, 176)], load_sem.at[2 + n])
+        olds.append(
+            pltpu.make_async_copy(old, state.at[n, pl.ds(96, 176)], load_sem.at[5 + n])
         )
-    for copy in loads:
+    for copy in loads + olds:
         copy.start()
 
     barrier = pltpu.get_barrier_semaphore()
@@ -94,29 +103,10 @@
 
     pl.semaphore_wait(barrier, 13)
 
-    swaps = [
-        remote(query.at[:, 1 - core], other.at[pl.ds(0, 64)], s0_send.at[0], s0_recv.at[0], sibling),
-        remote(gate.at[:, 1 - core], other.at[pl.ds(64, 128)], s0_send.at[1], s0_recv.at[1], sibling),
-    ]
     for copy in swaps:
         copy.start()
     sent += swaps
 
-    for n in range(3):
-        state[n, pl.ds(0, 96)] = jnp.zeros((96, LANE), F32)
-        state[n, pl.ds(272, 96)] = jnp.zeros((96, LANE), F32)
-    for copy in loads[2:]:
-        copy.wait()
-    first = bounds[0, 0] // LANE
-    last = bounds[0, 1] // LANE
-
-    def window(n, base):
-        rows = lax.broadcasted_iota(jnp.int32, (96, LANE), 0) + base
-        piece = state[n, pl.ds(jnp.clip(base - first + 96, 0, 272), 96)]
-        return jnp.where((rows >= first) & (rows < last), piece, 0.0)
-
-    for n in range(3):
-        passed[n] = window(n, (me + 1) * 96)
     hands_on = (core == 0) | (at[2] % 2 == 0)
     takes = (core == 1) | (at[2] % 2 == 1)
     handed = remote(
@@ -124,50 +114,103 @@
         sibling * (1 - core) + device(2, 1, 0) * core,
     )
 
+    flat0 = s0.reshape(192 * PITCH, LANE)
+    blocks0 = s0.reshape(4, 4, 4, 3, PITCH, LANE)
+    rows0 = pl.ds(0, BLK)
+    by_first = {}
+    for x in range(4):
+        for n in of_chunk[x]:
+            loads[n].wait()
+            swaps[n].wait_recv()
+
+        def pair(i, carry):
+            row = pl.multiple_of(48 * x + 16 * i, 16)
+            for j in range(BLK):
+                lanes = pl.ds(j * LANE, LANE)
+                both = mine[pl.ds(row, 16), lanes].astype(F32) + other[pl.ds(row, 16), lanes].astype(F32)
+                flat0[pl.ds(row * PITCH + j, 16, stride=PITCH), :] = both
+            return carry
+
+        lax.fori_loop(0, 3, pair, 0)
+        if stop == 0:
+            continue
+
+        @pl.when(at[0] != x)
+        def _(x=x):
+            by = (x - at[0] + 4) % 4
+            remote(
+                blocks0.at[x, :, :, 0, rows0], r1.at[0, by - 1],
+                s1_send.at[by - 1], s1_recv.at[by - 1], device(0, by, core),
+            ).start()
+
+        for by in (2, 1, 3):
+            n = 3 + x * 6 + by - 1
+            to_y, to_z = (at[1] + by) % 4, (at[2] + by) % 4
+            by_first[1, x, by] = remote(
+                blocks0.at[x, to_y, :, 1, rows0], r1.at[1, by - 1, x],
+                s1_send.at[n], s1_recv.at[n], device(1, by, core),
+            )
+            by_first[2, x, by] = remote(
+                blocks0.at[x, :, to_z, 2, rows0], r1.at[2, by - 1, x],
+                s1_send.at[n + 3], s1_recv.at[n + 3], device(2, by, core),
+            )
+            for p in (1, 2):
+                by_first[p, x, by].start()
+                sent.append(by_first[p, x, by])
+    for by in (1, 2, 3):
+        by_first[0, 0, by] = remote(
+            blocks0.at[0, :, :, 0, rows0], r1.at[0, by - 1],
+            s1_send.at[by - 1], s1_recv.at[by - 1], device(0, by, core),
+        )
+        if stop > 0:
+            sent.append(by_first[0, 0, by])
+
+    for n in range(3):
+        state[n, pl.ds(0, 96)] = jnp.zeros((96, LANE), F32)
+        state[n, pl.ds(272, 96)] = jnp.zeros((96, LANE), F32)
+    for copy in olds:
+        copy.wait()
+    first = bounds[0, 0] // LANE
+    last = bounds[0, 1] // LANE
+
+    def window(n, base):
+        rows = lax.broadcasted_iota(jnp.int32, (96, LANE), 0) + base
+        piece = state[n, pl.ds(jnp.clip(base - first + 96, 0, 272), 96)]
+        return jnp.where((rows >= first) & (rows < last), piece, 0.0)
+
+    for n in range(3):
+        passed[n] = window(n, (me + 1) * 96)
+
     @pl.when(hands_on)
     def _():
         handed.start()
 
-    for copy in loads[:2]:
-        copy.wait()
-    for copy in swaps:
-        copy.wait_recv()
-
-    def pair(i, carry):
-        i_x, i_y = i // 4, i % 4
-        for z in range(4):
-            to = (4 * i + z, i_y * 16 + z * 4 + i_x, z * 16 + i_x * 4 + i_y)
-            for p in range(3):
-                row = 12 * i + 3 * z + p
-                s0[p, to[p]] = mine[row].astype(F32) + other[row].astype(F32)
-        return carry
-
-    lax.fori_loop(0, 16, pair, 0)
+    for n, ref in enumerate((new_m, new_v, new_s)):
+        ref[...] = window(n, me * 96)
+
     if stop == 0:
         return finish(stop, sent, handed, hands_on, takes, new_m, new_v, new_s, weights, s0)
 
-    copies1 = {}
-    for by in (2, 1, 3):
-        for p in range(3):
-            a = ORDER[p][0]
-            copies1[p, by] = remote(
-                s0.at[p, pl.ds((at[a] + by) % 4 * 16, 16)], r1.at[p, by - 1],
-                s1_send.at[p * 3 + by - 1], s1_recv.at[p * 3 + by - 1], device(a, by, core),
-            )
-            copies1[p, by].start()
-            sent.append(copies1[p, by])
     copies2 = {}
     for p in range(3):
         a, b, _ = ORDER[p]
         for by in (1, 2, 3):
-            copies1[p, by].wait_recv()
-        own = at[a] * 16
-
-        def second(i, carry, p=p, own=own):
-            s1[p, i] = (s0[p, own + i] + r1[p, 0, i]) + (r1[p, 1, i] + r1[p, 2, i])
+            for x in (range(4) if p else (0,)):
+                by_first[p, x, by].wait_recv()
+
+        def second(i, carry, p=p):
+            for k in range(4):
+                if p == 0:
+                    own, to = (at[0], i, k, 0), i * 4 + k
+                elif p == 1:
+                    own, to = (i, at[1], k, 1), k * 4 + i
+                else:
+                    own, to = (i, k, at[2], 2), i * 4 + k
+                own = blocks0[own + (rows0,)]
+                s1[p, to] = (own + r1[p, 0, i, k]) + (r1[p, 1, i, k] + r1[p, 2, i, k])
             return carry
 
-        lax.fori_loop(0, 16, second, 0)
+        lax.fori_loop(0, 4, second, 0)
         if stop == 1:
             continue
         for by in (2, 1, 3):
@@ -228,9 +271,8 @@
     def _():
         arrived[...] = jnp.zeros_like(arrived)
 
-    own_state = [window(n, me * 96) + arrived[n] for n in range(3)]
     for n, ref in enumerate((new_m, new_v, new_s)):
-        ref[...] = own_state[n]
+        ref[...] += arrived[n]
 
     last_at = (
         at[2] * (1 - core) + at[0] * core,
@@ -339,29 +381,71 @@
             handed.wait_recv()
         for ref in (new_m, new_v, new_s):
             ref[...] = jnp.zeros_like(ref)
-        weights[0, 0, 0, 0] = s0[0, 0].astype(BF16)
+        weights[0, 0, 0, 0] = s0[0, pl.ds(0, BLK)].astype(BF16)
+
+
+def write(weights, new_m, new_v, new_s, query, gate, out_m, out_v, out_s, tiles, sems):
+    split, rows = query.shape[0], tiles.shape[0]
+    copies = [
+        pltpu.make_async_copy(src, dst, sems.at[rows // 16 + n])
+        for n, (src, dst) in enumerate(((new_m, out_m), (new_v, out_v), (new_s, out_s)))
+    ]
+
+    def group(i, carry):
+        at = pl.ds(pl.multiple_of(16 * i, 16), 16)
+        for j in range(0, weights.shape[1], 8):
+            block = jnp.swapaxes(weights[at, pl.ds(j, 8)], 0, 1)
+            for k in range(8):
+                tiles[at, pl.ds((j + k) * LANE, LANE)] = block[k]
+
+        @pl.when(i < split // 16)
+        def _():
+            pltpu.make_async_copy(tiles.at[at], query.at[at], sems.at[i]).start()
+
+        @pl.when(i >= split // 16)
+        def _():
+            to = pl.ds(pl.multiple_of(16 * i - split, 16), 16)
+            pltpu.make_async_copy(tiles.at[at], gate.at[to], sems.at[i]).start()
+
+        return carry
+
+    for copy in copies:
+        copy.start()
+    lax.fori_loop(0, rows // 16, group, 0)
+    for i in range(rows // 16):
+        to = query.at[pl.ds(16 * i, 16)] if 16 * i < split else gate.at[pl.ds(16 * i - split, 16)]
+        copies.append(pltpu.make_async_copy(tiles.at[pl.ds(16 * i, 16)], to, sems.at[i]))
+    for copy in copies:
+        copy.wait()
 
 
 def on_device(grad_query, grad_gate, old_master, old_moment, old_variance, old_bounds, stop=9):
     query_rows, row_width = grad_query.shape[1:]
     gate_rows = grad_gate.shape[1]
-    query = grad_query.reshape(query_rows, 2, BLK, LANE)
-    gate = grad_gate.reshape(gate_rows, 2, BLK, LANE)
+    query = grad_query.reshape(query_rows, row_width)
+    gate = grad_gate.reshape(gate_rows, row_width)
     old = [a.reshape(-1, LANE) for a in (old_master, old_moment, old_variance)]
-    any_space = pl.BlockSpec(memory_space=pl.ANY)
+    query, gate, *old = [
+        pltpu.with_memory_space_constraint(a, pltpu.HBM) for a in (query, gate, *old)
+    ]
+    hbm = pl.BlockSpec(memory_space=pltpu.HBM)
     vmem = pl.BlockSpec(memory_space=pltpu.VMEM)
     dma = pltpu.SemaphoreType.DMA
     shard = jax.ShapeDtypeStruct((96, LANE), F32)
+    rows = query_rows + gate_rows
     new_m, new_v, new_s, weights = pl.pallas_call(
         functools.partial(kernel, stop),
-        out_shape=(shard, shard, shard, jax.ShapeDtypeStruct((4, 4, 4, 6, BLK, LANE), BF16)),
-        in_specs=[any_space] * 5 + [pl.BlockSpec(memory_space=pltpu.SMEM)],
+        out_shape=(
+            pltpu.VMEM(shard.shape, F32), pltpu.VMEM(shard.shape, F32), pltpu.VMEM(shard.shape, F32),
+            pltpu.VMEM((4, 4, 4, 6, BLK, LANE), BF16),
+        ),
+        in_specs=[hbm] * 5 + [pl.BlockSpec(memory_space=pltpu.SMEM)],
         out_specs=(vmem, vmem, vmem, vmem),
         scratch_shapes=[
-            pltpu.VMEM((192, BLK, LANE), BF16),
-            pltpu.VMEM((192, BLK, LANE), BF16),
-            pltpu.VMEM((3, 64, BLK, LANE), F32),
-            pltpu.VMEM((3, 3, 16, BLK, LANE), F32),
+            pltpu.VMEM((rows, row_width // 2), BF16),
+            pltpu.VMEM((rows, row_width // 2), BF16),
+            pltpu.VMEM((rows, PITCH, LANE), F32),
+            pltpu.VMEM((3, 3, 4, 4, BLK, LANE), F32),
             pltpu.VMEM((3, 16, BLK, LANE), F32),
             pltpu.VMEM((3, 3, 4, BLK, LANE), F32),
             pltpu.VMEM((3, 4, BLK, LANE), F32),
@@ -369,9 +453,9 @@
             pltpu.VMEM((3, 368, LANE), F32),
             pltpu.VMEM((3, 96, LANE), F32),
             pltpu.VMEM((3, 96, LANE), F32),
-            dma((5,)),
-            dma((2,)), dma((2,)),
-            dma((9,)), dma((9,)),
+            dma((8,)),
+            dma((5,)), dma((5,)),
+            dma((27,)), dma((27,)),
             dma((9,)), dma((9,)),
             dma((12,)), dma((12,)),
             dma((1,)), dma((1,)),
@@ -380,16 +464,22 @@
             dma((1,)), dma((1,)),
         ],
         compiler_params=pltpu.CompilerParams(
-            collective_id=0, has_side_effects=True, vmem_limit_bytes=40 * 1024 * 1024
+            collective_id=0, has_side_effects=True, vmem_limit_bytes=48 * 1024 * 1024
         ),
     )(query, gate, *old, old_bounds)
-    flat = weights.reshape(-1)
-    split = query_rows * row_width
-    return (
-        new_m.reshape(-1), new_v.reshape(-1), new_s.reshape(-1),
-        flat[:split].reshape(query_rows, row_width),
-        flat[split:].reshape(gate_rows, row_width),
-    )
+    query_new, gate_new, new_m, new_v, new_s = pl.pallas_call(
+        write,
+        out_shape=(
+            jax.ShapeDtypeStruct((query_rows, row_width), BF16),
+            jax.ShapeDtypeStruct((gate_rows, row_width), BF16),
+            shard, shard, shard,
+        ),
+        in_specs=[vmem] * 4,
+        out_specs=(hbm,) * 5,
+        scratch_shapes=[pltpu.VMEM((rows, row_width), BF16), dma((rows // 16 + 3,))],
+        compiler_params=pltpu.CompilerParams(vmem_limit_bytes=48 * 1024 * 1024),
+    )(weights.reshape(rows, row_width // LANE, LANE), new_m, new_v, new_s)
+    return (new_m.reshape(-1), new_v.reshape(-1), new_s.reshape(-1), query_new, gate_new)
 
 
 def solution(mesh, stop=9):

time: 68 us -> 56.4 us (0.83)
  local copies, waits for them, and re-layouts: 13.4 us -> 0.65 us
  Pallas kernels: 53.7 us -> 55 us
    slice x3 -> x0, local copies, waits for them, and re-layouts: 8.68 us -> none  [the longest x2 5.58 us: on_device(): flat[:split].reshape(query_rows, row_width)]
    unnamed x15 -> x2, local copies, waits for them, and re-layouts: 4.73 us -> 0.65 us
    pallas_call x1 -> x2, Pallas kernels: 53.7 us -> 55 us  [the longest x1 53.1 us: on_device(): pl.pallas_call(functools.partial(kernel, stop), out_shape=(pltpu.VMEM(sha...]
where the time goes in v2:
time: 56.4 us; the launch traced here: 56.3 us
  Pallas kernels  55 us (98%)
  local copies, waits for them, and re-layouts  0.65 us (1%)
  between operations  0.65 us (1%)
    pallas_call x1, Pallas kernels, on_device(): pl.pallas_call(functools.partial(kernel, stop), out_shape=(pltpu.VMEM(sha...  53.1 us
    pallas_call x1, Pallas kernels, on_device(): pl.pallas_call(write, out_shape=(jax.ShapeDtypeStruct((query_rows, row_wi...  1.88 us

profile of v2, /device:TPU:1, one launch (start us, length us, event | category | flops | bytes accessed | tf_op | source)
XLA Modules:
  0.0 56.3 jit_solution(12504542290242249985)
XLA Ops:
  0.6 0.0 copy-start
  0.6 0.6 %copy-done = s32[1,2]{1,0:T(1,128)S(1)} copy-done((s32[1,2]{1,0:T(1,128)S(1)}, s32[1,2]{1,0:T(1,128)}, u32[]{:S(2)}) %copy-start) | copy-done | bytes 32
  1.3 53.1 %shard_map.101 = (f32[96,128]{1,0:T(8,128)S(1)}, f32[96,128]{1,0:T(8,128)S(1)}, f32[96,128]{1,0:T(8,128)S(1)}, bf16[4,4,4,6,32,128]{5,4,3,2,1,0:T(8,128)(2,1)S(1)}) custom-call(bf16[64,8192]{1,0:T(8,128)(2,1)} %bitcast.11, bf16[128,8192]{1,0:T(8,128)(2,1)} %bitcast.10, f32[176,128]{1,0:T(8,128)} %bitcast.12, f32[176,128]{1,0:T(8,128)} %bitcast.13, ...), custom_call_target="tpu_custom_call" | custom-call | tf_op jit(solution)/shard_map/pallas_call | solution.py:436
  54.4 1.9 %shard_map.102 = (bf16[64,8192]{1,0:T(8,128)(2,1)}, bf16[128,8192]{1,0:T(8,128)(2,1)}, f32[96,128]{1,0:T(8,128)}, f32[96,128]{1,0:T(8,128)}, f32[96,128]{1,0:T(8,128)}) custom-call(bf16[192,64,128]{2,1,0:T(8,128)(2,1)S(1)} %bitcast.9, f32[96,128]{1,0:T(8,128)S(1)} %get-tuple-element.15.new_m, f32[96,128]{1,0:T(8,128)S(1)} %get-tuple-element.16.new_v, ...), custom_call_target="tpu_custom_call" | custom-call | tf_op jit(solution)/shard_map/pallas_call | solution.py:470
Async XLA Ops:
  0.6 0.7 %copy-start = (s32[1,2]{1,0:T(1,128)S(1)}, s32[1,2]{1,0:T(1,128)}, u32[]{:S(2)}) copy-start(s32[1,2]{1,0:T(1,128)} %bounds.1) | copy-start | bytes 28

commit v3 on v2

--- a/solution.py
+++ b/solution.py
@@ -21,6 +21,7 @@
 LANE = 128
 PITCH = 40
 BLK = 32
+BOUND = (48.0, 192.0)
 ORDER = ((0, 1, 2), (1, 2, 0), (2, 0, 1))
 
 
@@ -35,11 +36,24 @@
     return (master_new, moment_new, variance_new)
 
 
+def encode(value, bound):
+    ratio = jnp.maximum(jnp.abs(value), 1e-30) * (1.0 / bound)
+    root = lax.rsqrt(lax.rsqrt(ratio))
+    code = root * lax.rsqrt(root) * 32767.0
+    return jnp.round(jnp.where(value < 0, -code, code)).astype(jnp.int32).astype(jnp.int16)
+
+
+def decode(code, bound):
+    root = code.astype(jnp.int32).astype(F32) * (bound**0.125 / 32767.0)
+    square = root * root
+    return (root * jnp.abs(root)) * (square * (square * square))
+
+
 def kernel(
     stop,
-    query, gate, old_m, old_v, old_s, bounds,
+    query, gate, old_m, old_v, old_s, bounds_hbm,
     new_m, new_v, new_s, weights,
-    mine, other, s0, r1, s1, r2, s2, r3, state, passed, arrived,
+    mine, other, s0, e0, r1, s1, e1, r2, s2, r3, state, passed, arrived, bounds,
     load_sem, s0_send, s0_recv, s1_send, s1_recv, s2_send, s2_recv, s3_send, s3_recv,
     x_send, x_recv, g_send, g_recv, c_send, c_recv, p_send, p_recv,
 ):
@@ -78,7 +92,8 @@
         olds.append(
             pltpu.make_async_copy(old, state.at[n, pl.ds(96, 176)], load_sem.at[5 + n])
         )
-    for copy in loads + olds:
+    olds.append(pltpu.make_async_copy(bounds_hbm, bounds, load_sem.at[8]))
+    for copy in olds + loads:
         copy.start()
 
     barrier = pltpu.get_barrier_semaphore()
@@ -100,6 +115,24 @@
     def _():
         for by in (1, 2, 3):
             greet(device(1, by, 0))
+
+    for n in range(3):
+        state[n, pl.ds(0, 96)] = jnp.zeros((96, LANE), F32)
+        state[n, pl.ds(272, 96)] = jnp.zeros((96, LANE), F32)
+    for copy in olds:
+        copy.wait()
+    first = bounds[0, 0] // LANE
+    last = bounds[0, 1] // LANE
+
+    def window(n, base):
+        rows = lax.broadcasted_iota(jnp.int32, (96, LANE), 0) + base
+        piece = state[n, pl.ds(jnp.clip(base - first + 96, 0, 272), 96)]
+        return jnp.where((rows >= first) & (rows < last), piece, 0.0)
+
+    for n in range(3):
+        passed[n] = window(n, (me + 1) * 96)
+    for n, ref in enumerate((new_m, new_v, new_s)):
+        ref[...] = window(n, me * 96)
 
     pl.semaphore_wait(barrier, 13)
 
@@ -113,6 +146,10 @@
         passed, arrived, p_send.at[0], p_recv.at[0],
         sibling * (1 - core) + device(2, 1, 0) * core,
     )
+
+    @pl.when(hands_on)
+    def _():
+        handed.start()
 
     flat0 = s0.reshape(192 * PITCH, LANE)
     blocks0 = s0.reshape(4, 4, 4, 3, PITCH, LANE)
@@ -137,56 +174,42 @@
 
         @pl.when(at[0] != x)
         def _(x=x):
+            def code(i, carry):
+                for k in range(4):
+                    e0[0, x, i, k] = encode(blocks0[x, i, k, 0, rows0], BOUND[0])
+                return carry
+
+            lax.fori_loop(0, 4, code, 0)
             by = (x - at[0] + 4) % 4
             remote(
-                blocks0.at[x, :, :, 0, rows0], r1.at[0, by - 1],
+                e0.at[0, x], r1.at[0, by - 1],
                 s1_send.at[by - 1], s1_recv.at[by - 1], device(0, by, core),
             ).start()
 
+        def code(i, carry, x=x):
+            for by in (1, 2, 3):
+                to_y, to_z = (at[1] + by) % 4, (at[2] + by) % 4
+                e0[1, to_y, x, i] = encode(blocks0[x, to_y, i, 1, rows0], BOUND[0])
+                e0[2, to_z, x, i] = encode(blocks0[x, i, to_z, 2, rows0], BOUND[0])
+            return carry
+
+        lax.fori_loop(0, 4, code, 0)
         for by in (2, 1, 3):
             n = 3 + x * 6 + by - 1
-            to_y, to_z = (at[1] + by) % 4, (at[2] + by) % 4
-            by_first[1, x, by] = remote(
-                blocks0.at[x, to_y, :, 1, rows0], r1.at[1, by - 1, x],
-                s1_send.at[n], s1_recv.at[n], device(1, by, core),
-            )
-            by_first[2, x, by] = remote(
-                blocks0.at[x, :, to_z, 2, rows0], r1.at[2, by - 1, x],
-                s1_send.at[n + 3], s1_recv.at[n + 3], device(2, by, core),
-            )
             for p in (1, 2):
+                by_first[p, x, by] = remote(
+                    e0.at[p, (at[p] + by) % 4, x], r1.at[p, by - 1, x],
+                    s1_send.at[n + 3 * p - 3], s1_recv.at[n + 3 * p - 3], device(p, by, core),
+                )
                 by_first[p, x, by].start()
                 sent.append(by_first[p, x, by])
     for by in (1, 2, 3):
         by_first[0, 0, by] = remote(
-            blocks0.at[0, :, :, 0, rows0], r1.at[0, by - 1],
+            e0.at[0, 0], r1.at[0, by - 1],
             s1_send.at[by - 1], s1_recv.at[by - 1], device(0, by, core),
         )
         if stop > 0:
             sent.append(by_first[0, 0, by])
-
-    for n in range(3):
-        state[n, pl.ds(0, 96)] = jnp.zeros((96, LANE), F32)
-        state[n, pl.ds(272, 96)] = jnp.zeros((96, LANE), F32)
-    for copy in olds:
-        copy.wait()
-    first = bounds[0, 0] // LANE
-    last = bounds[0, 1] // LANE
-
-    def window(n, base):
-        rows = lax.broadcasted_iota(jnp.int32, (96, LANE), 0) + base
-        piece = state[n, pl.ds(jnp.clip(base - first + 96, 0, 272), 96)]
-        return jnp.where((rows >= first) & (rows < last), piece, 0.0)
-
-    for n in range(3):
-        passed[n] = window(n, (me + 1) * 96)
-
-    @pl.when(hands_on)
-    def _():
-        handed.start()
-
-    for n, ref in enumerate((new_m, new_v, new_s)):
-        ref[...] = window(n, me * 96)
 
     if stop == 0:
         return finish(stop, sent, handed, hands_on, takes, new_m, new_v, new_s, weights, s0)
@@ -206,8 +229,11 @@
                     own, to = (i, at[1], k, 1), k * 4 + i
                 else:
                     own, to = (i, k, at[2], 2), i * 4 + k
-                own = blocks0[own + (rows0,)]
-                s1[p, to] = (own + r1[p, 0, i, k]) + (r1[p, 1, i, k] + r1[p, 2, i, k])
+                total = blocks0[own + (rows0,)]
+                for by in range(3):
+                    total += decode(r1[p, by, i, k], BOUND[0])
+                s1[p, to] = total
+                e1[p, to] = encode(total, BOUND[1])
             return carry
 
         lax.fori_loop(0, 4, second, 0)
@@ -215,7 +241,7 @@
             continue
         for by in (2, 1, 3):
             copies2[p, by] = remote(
-                s1.at[p, pl.ds((at[b] + by) % 4 * 4, 4)], r2.at[p, by - 1],
+                e1.at[p, pl.ds((at[b] + by) % 4 * 4, 4)], r2.at[p, by - 1],
                 s2_send.at[p * 3 + by - 1], s2_recv.at[p * 3 + by - 1], device(b, by, core),
             )
             copies2[p, by].start()
@@ -229,7 +255,10 @@
             copies2[p, by].wait_recv()
         for i in range(4):
             own = at[b] * 4 + i
-            s2[p, i] = (s1[p, own] + r2[p, 0, i]) + (r2[p, 1, i] + r2[p, 2, i])
+            total = s1[p, own]
+            for by in range(3):
+                total += decode(r2[p, by, i], BOUND[1])
+            s2[p, i] = total
         if stop == 2:
             continue
         unit = 2 * p + core
@@ -317,49 +346,57 @@
         place[axis] = (place[axis] - by) % 4
         return place
 
-    def await_slab(m, free, axis, by, sem):
-        src = slab(m, free, moved(axis, by))
+    def await_slab(m, free, where, sem):
+        src = slab(m, free, where)
         remote(src, src, g_send.at[0], sem, sibling).wait_recv()
 
-    for level in (1, 2):
+    def forward(m, by, block):
+        copy = remote(block, block, c_send.at[m * 4 + by], c_recv.at[m * 4 + by], sibling)
+        copy.start()
+        sent.append(copy)
+
+    def last_level(m, group):
+        a, b, c = ORDER[m]
+        block = slab(m, (c,), moved(b, group))
+        for by in (2, 1, 3):
+            number = 18 + m * 12 + group * 3 + by - 1
+            copy = remote(
+                block, block, g_send.at[number], g_recv.at[number], device(a, by, core)
+            )
+            copy.start()
+            sent.append(copy)
+
+    for m in range(3):
+        a, b, c = ORDER[m]
+        for by in (1, 2, 3):
+            await_slab(m, (), moved(c, by), g_recv.at[m * 3 + by - 1])
+        block = slab(m, (c,), at)
+        for by in (2, 1, 3):
+            number = 9 + m * 3 + by - 1
+            copy = remote(
+                block, block, g_send.at[number], g_recv.at[number], device(b, by, core)
+            )
+            copy.start()
+            sent.append(copy)
+        last_level(m, 0)
+    for group in (1, 3, 2):
         for m in range(3):
             a, b, c = ORDER[m]
-            before, axis = ((c, b) if level == 1 else (b, a))
-            held = () if level == 1 else (c,)
-            for by in (1, 2, 3):
-                await_slab(m, held, before, by, g_recv.at[(level - 1) * 9 + m * 3 + by - 1])
-            free = held + (before,)
-            block = slab(m, free, at)
-            for by in (2, 1, 3):
-                number = level * 9 + m * 3 + by - 1
-                copy = remote(
-                    block, block, g_send.at[number], g_recv.at[number], device(axis, by, core)
-                )
-                copy.start()
-                sent.append(copy)
-            if level == 2:
-                copy = remote(block, block, c_send.at[m * 4], c_recv.at[m * 4], sibling)
-                copy.start()
-                sent.append(copy)
-    if stop == 4:
-        for m in range(3):
-            a, b, c = ORDER[m]
-            for by in (1, 2, 3):
-                await_slab(m, (b, c), a, by, g_recv.at[18 + m * 3 + by - 1])
-            src = slab(m, (b, c), at)
-            remote(src, src, c_send.at[0], c_recv.at[m * 4], sibling).wait_recv()
-        return finish(stop, sent, handed, hands_on, takes, new_m, new_v, new_s, weights, s0)
+            await_slab(m, (c,), moved(b, group), g_recv.at[9 + m * 3 + group - 1])
+            last_level(m, group)
+    for m in range(3):
+        forward(m, 0, slab(m, ORDER[m][1:], at))
     for by in (1, 3, 2):
         for m in range(3):
             a, b, c = ORDER[m]
-            await_slab(m, (b, c), a, by, g_recv.at[18 + m * 3 + by - 1])
-            block = slab(m, (b, c), moved(a, by))
-            copy = remote(block, block, c_send.at[m * 4 + by], c_recv.at[m * 4 + by], sibling)
-            copy.start()
-            sent.append(copy)
-    for m in range(3):
-        a, b, c = ORDER[m]
-        for by in range(4):
+            for group in (0, 1, 3, 2):
+                place = moved(a, by)
+                place[b] = (place[b] - group) % 4
+                await_slab(m, (c,), place, g_recv.at[18 + m * 12 + group * 3 + by - 1])
+            forward(m, by, slab(m, (b, c), moved(a, by)))
+    for by in (0, 1, 3, 2):
+        for m in range(3):
+            a, b, c = ORDER[m]
             index = moved(a, by)
             index = [slice(None) if axis in (b, c) else index[axis] for axis in range(3)]
             src = weights.at[index[0], index[1], index[2], 3 * (1 - core) + m]
@@ -425,8 +462,8 @@
     query = grad_query.reshape(query_rows, row_width)
     gate = grad_gate.reshape(gate_rows, row_width)
     old = [a.reshape(-1, LANE) for a in (old_master, old_moment, old_variance)]
-    query, gate, *old = [
-        pltpu.with_memory_space_constraint(a, pltpu.HBM) for a in (query, gate, *old)
+    query, gate, *old, old_bounds = [
+        pltpu.with_memory_space_constraint(a, pltpu.HBM) for a in (query, gate, *old, old_bounds)
     ]
     hbm = pl.BlockSpec(memory_space=pltpu.HBM)
     vmem = pl.BlockSpec(memory_space=pltpu.VMEM)
@@ -439,27 +476,30 @@
             pltpu.VMEM(shard.shape, F32), pltpu.VMEM(shard.shape, F32), pltpu.VMEM(shard.shape, F32),
             pltpu.VMEM((4, 4, 4, 6, BLK, LANE), BF16),
         ),
-        in_specs=[hbm] * 5 + [pl.BlockSpec(memory_space=pltpu.SMEM)],
+        in_specs=[hbm] * 6,
         out_specs=(vmem, vmem, vmem, vmem),
         scratch_shapes=[
             pltpu.VMEM((rows, row_width // 2), BF16),
             pltpu.VMEM((rows, row_width // 2), BF16),
             pltpu.VMEM((rows, PITCH, LANE), F32),
-            pltpu.VMEM((3, 3, 4, 4, BLK, LANE), F32),
+            pltpu.VMEM((3, 4, 4, 4, BLK, LANE), jnp.int16),
+            pltpu.VMEM((3, 3, 4, 4, BLK, LANE), jnp.int16),
             pltpu.VMEM((3, 16, BLK, LANE), F32),
-            pltpu.VMEM((3, 3, 4, BLK, LANE), F32),
+            pltpu.VMEM((3, 16, BLK, LANE), jnp.int16),
+            pltpu.VMEM((3, 3, 4, BLK, LANE), jnp.int16),
             pltpu.VMEM((3, 4, BLK, LANE), F32),
             pltpu.VMEM((3, 4, BLK, LANE), F32),
             pltpu.VMEM((3, 368, LANE), F32),
             pltpu.VMEM((3, 96, LANE), F32),
             pltpu.VMEM((3, 96, LANE), F32),
-            dma((8,)),
+            pltpu.SMEM((1, 2), jnp.int32),
+            dma((9,)),
             dma((5,)), dma((5,)),
             dma((27,)), dma((27,)),
             dma((9,)), dma((9,)),
             dma((12,)), dma((12,)),
             dma((1,)), dma((1,)),
-            dma((27,)), dma((27,)),
+            dma((54,)), dma((54,)),
             dma((12,)), dma((12,)),
             dma((1,)), dma((1,)),
         ],

time: 56.4 us -> 48.9 us (0.87)
  Pallas kernels: 55 us -> 48.2 us
  local copies, waits for them, and re-layouts: 0.65 us -> 0 us
    pallas_call x1, Pallas kernels: 53.1 us -> 46.3 us  [on_device(): pl.pallas_call(functools.partial(kernel, stop), out_shape=(pltpu.VMEM(sha...]
    unnamed x2 -> x0, local copies, waits for them, and re-layouts: 0.65 us -> none
where the time goes in v3:
time: 48.9 us; the launch traced here: 48.8 us
  Pallas kernels  48.2 us (99%)
  between operations  0.64 us (1%)
    pallas_call x1, Pallas kernels, on_device(): pl.pallas_call(functools.partial(kernel, stop), out_shape=(pltpu.VMEM(sha...  46.3 us
    pallas_call x1, Pallas kernels, on_device(): pl.pallas_call(write, out_shape=(jax.ShapeDtypeStruct((query_rows, row_wi...  1.88 us

profile of v3, /device:TPU:1, one launch (start us, length us, event | category | flops | bytes accessed | tf_op | source)
XLA Modules:
  0.0 48.8 jit_solution(677574426437123327)
XLA Ops:
  0.6 46.3 %shard_map.101 = (f32[96,128]{1,0:T(8,128)S(1)}, f32[96,128]{1,0:T(8,128)S(1)}, f32[96,128]{1,0:T(8,128)S(1)}, bf16[4,4,4,6,32,128]{5,4,3,2,1,0:T(8,128)(2,1)S(1)}) custom-call(bf16[64,8192]{1,0:T(8,128)(2,1)} %bitcast.11, bf16[128,8192]{1,0:T(8,128)(2,1)} %bitcast.10, f32[176,128]{1,0:T(8,128)} %bitcast.12, f32[176,128]{1,0:T(8,128)} %bitcast.13, ...), custom_call_target="tpu_custom_call" | custom-call | tf_op jit(solution)/shard_map/pallas_call | solution.py:473
  46.9 1.9 %shard_map.102 = (bf16[64,8192]{1,0:T(8,128)(2,1)}, bf16[128,8192]{1,0:T(8,128)(2,1)}, f32[96,128]{1,0:T(8,128)}, f32[96,128]{1,0:T(8,128)}, f32[96,128]{1,0:T(8,128)}) custom-call(bf16[192,64,128]{2,1,0:T(8,128)(2,1)S(1)} %bitcast.9, f32[96,128]{1,0:T(8,128)S(1)} %get-tuple-element.15.new_m, f32[96,128]{1,0:T(8,128)S(1)} %get-tuple-element.16.new_v, ...), custom_call_target="tpu_custom_call" | custom-call | tf_op jit(solution)/shard_map/pallas_call | solution.py:510

commit v4 on v0

v4 whole, which is shorter than its diff:
```python
import functools

import jax
import jax.numpy as jnp
from jax import lax
from jax.experimental import pallas as pl
from jax.experimental.pallas import tpu as pltpu
from jax.sharding import PartitionSpec as P

MESH = pl.DeviceIdType.MESH
F32 = jnp.float32
BF16 = jnp.bfloat16

STEP = 10
beta_one = 0.9
beta_two = 0.95
learn_rate = 0.01
decay_rate = 0.1
epsilon = 1e-08

LANE = 128
BLK = 32
HALF = 16
PITCH = 24
BOUND = (48.0, 192.0)
TURNS = (0, 1, 3, 2)
AWAY = ((2, 2), (2, 1), (1, 2), (2, -1), (-1, 2), (1, 1), (1, -1), (-1, 1), (-1, -1),
        (2, 0), (0, 2), (1, 0), (0, 1), (-1, 0), (0, -1))
ORDER = ((0, 1, 2), (1, 2, 0), (2, 0, 1))


def adamw_step(master, moment, variance, grad):
    moment_new = beta_one * moment + (1.0 - beta_one) * grad
    variance_new = beta_two * variance + (1.0 - beta_two) * grad * grad
    corrected_m = moment_new / (1.0 - beta_one**STEP)
    corrected_v = variance_new / (1.0 - beta_two**STEP)
    master_new = master - learn_rate * (
        corrected_m / (jnp.sqrt(corrected_v) + epsilon) + decay_rate * master
    )
    return (master_new, moment_new, variance_new)


def encode(value, bound):
    ratio = jnp.maximum(jnp.abs(value), 1e-30) * (1.0 / bound)
    root = lax.rsqrt(lax.rsqrt(ratio))
    code = root * lax.rsqrt(root) * 32767.0
    return jnp.round(jnp.where(value < 0, -code, code)).astype(jnp.int32).astype(jnp.int16)


def decode(code, bound):
    root = code.astype(jnp.int32).astype(F32) * (bound**0.125 / 32767.0)
    square = root * root
    return (root * jnp.abs(root)) * (square * (square * square))


def kernel(
    stop,
    query, gate, old_m, old_v, old_s, bounds_hbm,
    new_m, new_v, new_s, weights,
    mine, other, s0, e0, r0, s1, e1, r1, state, passed, arrived, bounds,
    load_sem, near_sem, send_sem, s0_recv, s1_recv, s2_recv, g1_recv, g2_recv, g3_recv, c_recv, p_recv,
):
    me = lax.axis_index("dp")
    core = me % 2
    chip = me // 2
    at = (chip // 16, (chip // 4) % 4, chip % 4)
    sibling = me + 1 - 2 * core

    def device(moves, on_core):
        place = [(at[axis] + moves.get(axis, 0)) % 4 for axis in range(3)]
        return ((place[0] * 4 + place[1]) * 4 + place[2]) * 2 + on_core

    def remote(src, dst, send, recv, to):
        return pltpu.make_async_remote_copy(
            src_ref=src, dst_ref=dst, send_sem=send, recv_sem=recv,
            device_id=(to,), device_id_type=MESH,
        )

    over = []

    def start(src, dst, send, recv, to):
        remote(src, dst, send_sem.at[send], recv, to).start()

    def await_from(dst, recv):
        remote(dst, dst, send_sem.at[0], recv, sibling).wait_recv()

    def done():
        totals = (
            other, e0.at[:, :, pl.ds(0, 3)], e1.at[:, pl.ds(0, 15)],
            weights.at[0, 0, pl.ds(0, 3), pl.ds(0, 3)], weights.at[0, pl.ds(0, 3), :, pl.ds(0, 3)],
            weights.at[pl.ds(0, 3), :, :, pl.ds(0, 3)], weights.at[:, :, :, pl.ds(0, 3)],
        )
        for n in range({0: 1, 1: 2, 3: 3}.get(stop, 7)):
            remote(totals[n], totals[n], send_sem.at[n], s0_recv.at[0], sibling).wait_send()
        for crosses, across in over:
            @pl.when(crosses)
            def _(across=across):
                across.wait_send()

        @pl.when(hands_on)
        def _():
            handed.wait_send()

        if 0 <= stop < 3:
            @pl.when(takes)
            def _():
                handed.wait_recv()

    wide = mine.shape[2]
    split = query.shape[0]
    loads, olds, swaps = [], [], []
    for g in range(2):
        own_half = pl.ds(pl.multiple_of((2 * core + g) * wide, wide), wide)
        its_half = pl.ds(pl.multiple_of((2 - 2 * core + g) * wide, wide), wide)
        for n, (array, rows) in enumerate(((query, pl.ds(0, split)), (gate, pl.ds(split, gate.shape[0])))):
            loads.append(pltpu.make_async_copy(
                array.at[:, own_half], mine.at[g, rows], load_sem.at[g]))
            swaps.append(remote(
                array.at[:, its_half], other.at[g, rows], send_sem.at[0], s0_recv.at[g], sibling))
    for n, old in enumerate((old_m, old_v, old_s)):
        olds.append(
            pltpu.make_async_copy(old, state.at[n, pl.ds(96, 176)], load_sem.at[2])
        )
    olds.append(pltpu.make_async_copy(bounds_hbm, bounds, load_sem.at[3]))
    for copy in olds + loads:
        copy.start()

    barrier = pltpu.get_barrier_semaphore()
    around = [sibling] + [device({axis: by}, core) for axis in range(3) for by in (1, 3)]

    def greet(sem):
        for to in around:
            pl.semaphore_signal(sem, inc=1, device_id=(to,), device_id_type=MESH)

    greet(barrier)

    for n in range(3):
        state[n, pl.ds(0, 96)] = jnp.zeros((96, LANE), F32)
        state[n, pl.ds(272, 96)] = jnp.zeros((96, LANE), F32)
    olds[-1].wait()
    whole = state.at[:, pl.ds(96, 176)]
    pltpu.make_async_copy(whole, whole, load_sem.at[2]).wait()
    first = bounds[0, 0] // LANE
    last = bounds[0, 1] // LANE

    def window(n, base):
        rows = lax.broadcasted_iota(jnp.int32, (96, LANE), 0) + base
        piece = state[n, pl.ds(jnp.clip(base - first + 96, 0, 272), 96)]
        return jnp.where((rows >= first) & (rows < last), piece, 0.0)

    for n in range(3):
        passed[n] = window(n, (me + 1) * 96)
    for n, ref in enumerate((new_m, new_v, new_s)):
        ref[...] = window(n, me * 96)

    pl.semaphore_wait(barrier, len(around))

    for copy in swaps:
        copy.start()
    greet(near_sem.at[0])

    hands_on = (core == 0) | (at[2] % 2 == 0)
    takes = (core == 1) | (at[2] % 2 == 1)
    handed = remote(
        passed, arrived, send_sem.at[7], p_recv.at[0],
        sibling * (1 - core) + device({2: 1}, 0) * core,
    )

    def round_of(n):
        pl.semaphore_wait(near_sem.at[n], len(around))
        if n < 3:
            greet(near_sem.at[n + 1])

    flat0 = s0.reshape(2 * 192 * PITCH, LANE)
    blocks0 = s0.reshape(2, 4, 4, 4, 3, PITCH, LANE)
    rows0 = pl.ds(0, HALF)

    def block(p, g, a, b, c):
        place = [None] * 3
        for axis, value in zip(ORDER[p], (a, b, c)):
            place[axis] = value
        return blocks0[g, place[0], place[1], place[2], p, rows0]

    def slab_out(p, g, by):
        a = (at[ORDER[p][0]] + by) % 4

        def code(b, carry):
            for c in range(4):
                e0[p, g, a, b, c] = encode(block(p, g, a, b, c), BOUND[0])
            return carry

        lax.fori_loop(0, 4, code, 0)
        start(
            e0.at[p, g, a], r0.at[p, g, by - 1], 1, s1_recv.at[(p * 2 + g) * 3 + by - 1],
            device({ORDER[p][0]: by}, core),
        )

    for g in range(2):
        pltpu.make_async_copy(mine.at[g], mine.at[g], load_sem.at[g]).wait()
        await_from(other.at[g], s0_recv.at[g])

        def pair(i, carry, g=g):
            row = pl.multiple_of(16 * i, 16)
            for j in range(HALF):
                lanes = pl.ds(j * LANE, LANE)
                both = mine[g, pl.ds(row, 16), lanes].astype(F32) + other[g, pl.ds(row, 16), lanes].astype(F32)
                flat0[pl.ds((g * 192 + row) * PITCH + j, 16, stride=PITCH), :] = both
            return carry

        lax.fori_loop(0, 12, pair, 0)
        for by in (1, 3, 2):
            if by == 2:
                round_of(g)
            for p in range(3):
                if stop != 0:
                    slab_out(p, g, by)
        if g == 0:
            @pl.when(hands_on)
            def _():
                handed.start()
    round_of(2)
    if stop == 0:
        round_of(3)
        return done()

    for g in range(2):
        for p in range(3):
            for by in (1, 3):
                await_from(r0.at[p, g, by - 1], s1_recv.at[(p * 2 + g) * 3 + by - 1])

            def gather_one(b, carry, p=p, g=g):
                for c in range(4):
                    s1[p, b, c] = block(p, g, at[ORDER[p][0]], b, c) + (
                        decode(r0[p, g, 0, b, c], BOUND[0]) + decode(r0[p, g, 2, b, c], BOUND[0]))
                return carry

            lax.fori_loop(0, 4, gather_one, 0)
        if g == 1:
            round_of(3)
        for p in range(3):
            await_from(r0.at[p, g, 1], s1_recv.at[(p * 2 + g) * 3 + 1])

            def gather_two(b, carry, p=p, g=g):
                for c in range(4):
                    total = s1[p, b, c] + decode(r0[p, g, 1, b, c], BOUND[0])
                    e1[p, b * 4 + c, pl.ds(g * HALF, HALF)] = encode(total, BOUND[1])
                return carry

            lax.fori_loop(0, 4, gather_two, 0)
            if g == 0 or stop == 1:
                continue
            _, b, c = ORDER[p]
            unit = 2 * p + core
            owner = unit // 3
            place = unit % 3
            source = at[b] * 4 + at[c]
            for db, dc in AWAY:
                start(
                    e1.at[p, (at[b] + db) % 4 * 4 + (at[c] + dc) % 4], r1.at[place, source],
                    2, s2_recv.at[place], device({b: db, c: dc}, owner),
                )
            if p == 1:
                r1[place, source] = e1[p, source]
            else:
                across = remote(
                    e1.at[p, source], r1.at[place, source], send_sem.at[8], s2_recv.at[place], sibling,
                )
                crosses = core == (1 if p == 0 else 0)

                @pl.when(crosses)
                def _(across=across):
                    across.start()

                over.append((crosses, across))

                @pl.when(jnp.logical_not(crosses))
                def _(p=p, place=place, source=source):
                    r1[place, source] = e1[p, source]
    if stop == 1:
        return done()

    @pl.when(takes)
    def _():
        handed.wait_recv()

    @pl.when(jnp.logical_not(takes))
    def _():
        arrived[...] = jnp.zeros_like(arrived)

    for n, ref in enumerate((new_m, new_v, new_s)):
        ref[...] += arrived[n]

    for m in range(3):
        await_from(r1.at[m, pl.ds(0, 16 if m == 1 else 15)], s2_recv.at[m])
        values = [decode(r1[m, n], BOUND[1]) for n in range(16)]
        while len(values) > 1:
            values = [one + two for one, two in zip(values[::2], values[1::2])]
        total = values[0]
        rows = pl.ds(m * BLK, BLK)
        master, moment, variance = adamw_step(new_m[rows], new_v[rows], new_s[rows], total)
        new_m[rows] = master
        new_v[rows] = moment
        new_s[rows] = variance
        weights[at[0], at[1], at[2], 3 * core + m] = master.astype(BF16)
        if stop == 3:
            continue
        _, b, c = ORDER[m]
        own = weights.at[at[0], at[1], at[2], 3 * core + m]
        for by in (2, 1, 3):
            start(own, own, 3, g1_recv.at[m], device({c: by}, core))
    if stop == 3:
        return done()

    def slab(m, moves, free, on_core):
        index = [(at[axis] + moves.get(axis, 0)) % 4 for axis in range(3)]
        for axis in free:
            index[axis] = slice(None)
        return weights.at[index[0], index[1], index[2], 3 * on_core + m]

    def forward(m, moves, free):
        part = slab(m, moves, free, core)
        start(part, part, 6, c_recv.at[0], sibling)

    def group_out(m, turn):
        a, b, c = ORDER[m]
        part = slab(m, {b: -TURNS[turn]}, (c,), core)
        for by in (2, 1, 3):
            start(
                part, part, 5, g3_recv.at[m * 6 + (by - 1) * 2 + turn // 2], device({a: by}, core)
            )

    for m in range(3):
        a, b, c = ORDER[m]
        await_from(weights.at[0, 0, pl.ds(0, 3), m], g1_recv.at[m])
        part = slab(m, {}, (c,), core)
        for by in (2, 1, 3):
            start(part, part, 4, g2_recv.at[m * 3 + by - 1], device({b: by}, core))
        group_out(m, 0)
    for turn in (1, 2, 3):
        for m in range(3):
            a, b, c = ORDER[m]
            by = TURNS[turn]
            await_from(slab(m, {b: -by}, (c,), core), g2_recv.at[m * 3 + by - 1])
            group_out(m, turn)
    for m in range(3):
        forward(m, {}, ORDER[m][1:])
    for part in range(2):
        for by in (1, 3, 2):
            for m in range(3):
                a, b, c = ORDER[m]
                await_from(weights.at[0, pl.ds(0, 2), :, m], g3_recv.at[m * 6 + (by - 1) * 2 + part])
                for turn in (2 * part, 2 * part + 1):
                    forward(m, {a: -by, b: -TURNS[turn]}, (c,))
    await_from(weights.at[:, :, :, pl.ds(0, 3)], c_recv.at[0])
    done()


def write(weights, new_m, new_v, new_s, query, gate, out_m, out_v, out_s, tiles, sems):
    split, rows = query.shape[0], tiles.shape[0]
    copies = [
        pltpu.make_async_copy(src, dst, sems.at[rows // 16 + n])
        for n, (src, dst) in enumerate(((new_m, out_m), (new_v, out_v), (new_s, out_s)))
    ]

    def group(i, carry):
        at = pl.ds(pl.multiple_of(16 * i, 16), 16)
        for j in range(0, weights.shape[1], 8):
            block = jnp.swapaxes(weights[at, pl.ds(j, 8)], 0, 1)
            for k in range(8):
                tiles[at, pl.ds((j + k) * LANE, LANE)] = block[k]

        @pl.when(i < split // 16)
        def _():
            pltpu.make_async_copy(tiles.at[at], query.at[at], sems.at[i]).start()

        @pl.when(i >= split // 16)
        def _():
            to = pl.ds(pl.multiple_of(16 * i - split, 16), 16)
            pltpu.make_async_copy(tiles.at[at], gate.at[to], sems.at[i]).start()

        return carry

    for copy in copies:
        copy.start()
    lax.fori_loop(0, rows // 16, group, 0)
    for i in range(rows // 16):
        to = query.at[pl.ds(16 * i, 16)] if 16 * i < split else gate.at[pl.ds(16 * i - split, 16)]
        copies.append(pltpu.make_async_copy(tiles.at[pl.ds(16 * i, 16)], to, sems.at[i]))
    for copy in copies:
        copy.wait()


def on_device(grad_query, grad_gate, old_master, old_moment, old_variance, old_bounds, stop=9):
    query_rows, row_width = grad_query.shape[1:]
    gate_rows = grad_gate.shape[1]
    query = grad_query.reshape(query_rows, row_width)
    gate = grad_gate.reshape(gate_rows, row_width)
    old = [a.reshape(-1, LANE) for a in (old_master, old_moment, old_variance)]
    query, gate, *old, old_bounds = [
        pltpu.with_memory_space_constraint(a, pltpu.HBM) for a in (query, gate, *old, old_bounds)
    ]
    hbm = pl.BlockSpec(memory_space=pltpu.HBM)
    vmem = pl.BlockSpec(memory_space=pltpu.VMEM)
    dma = pltpu.SemaphoreType.DMA
    shard = jax.ShapeDtypeStruct((96, LANE), F32)
    rows = query_rows + gate_rows
    new_m, new_v, new_s, weights = pl.pallas_call(
        functools.partial(kernel, stop),
        out_shape=(
            pltpu.VMEM(shard.shape, F32), pltpu.VMEM(shard.shape, F32), pltpu.VMEM(shard.shape, F32),
            pltpu.VMEM((4, 4, 4, 6, BLK, LANE), BF16),
        ),
        in_specs=[hbm] * 6,
        out_specs=(vmem, vmem, vmem, vmem),
        scratch_shapes=[
            pltpu.VMEM((2, rows, row_width // 4), BF16),
            pltpu.VMEM((2, rows, row_width // 4), BF16),
            pltpu.VMEM((2, rows, PITCH, LANE), F32),
            pltpu.VMEM((3, 2, 4, 4, 4, HALF, LANE), jnp.int16),
            pltpu.VMEM((3, 2, 3, 4, 4, HALF, LANE), jnp.int16),
            pltpu.VMEM((3, 4, 4, HALF, LANE), F32),
            pltpu.VMEM((3, 16, BLK, LANE), jnp.int16),
            pltpu.VMEM((3, 16, BLK, LANE), jnp.int16),
            pltpu.VMEM((3, 368, LANE), F32),
            pltpu.VMEM((3, 96, LANE), F32),
            pltpu.VMEM((3, 96, LANE), F32),
            pltpu.SMEM((1, 2), jnp.int32),
            dma((4,)),
            pltpu.SemaphoreType.REGULAR((4,)),
            dma((9,)),
            dma((2,)), dma((18,)), dma((3,)),
            dma((3,)), dma((9,)), dma((18,)), dma((1,)), dma((1,)),
        ],
        compiler_params=pltpu.CompilerParams(
            collective_id=0, has_side_effects=True, vmem_limit_bytes=48 * 1024 * 1024
        ),
    )(query, gate, *old, old_bounds)
    query_new, gate_new, new_m, new_v, new_s = pl.pallas_call(
        write,
        out_shape=(
            jax.ShapeDtypeStruct((query_rows, row_width), BF16),
            jax.ShapeDtypeStruct((gate_rows, row_width), BF16),
            shard, shard, shard,
        ),
        in_specs=[vmem] * 4,
        out_specs=(hbm,) * 5,
        scratch_shapes=[pltpu.VMEM((rows, row_width), BF16), dma((rows // 16 + 3,))],
        compiler_params=pltpu.CompilerParams(vmem_limit_bytes=48 * 1024 * 1024),
    )(weights.reshape(rows, row_width // LANE, LANE), new_m, new_v, new_s)
    return (new_m.reshape(-1), new_v.reshape(-1), new_s.reshape(-1), query_new, gate_new)


def solution(mesh, stop=9):
    placed = (P("dp", None, None), P("dp", None, None), P("dp"), P("dp"), P("dp"), P("dp", None))
    return jax.shard_map(
        functools.partial(on_device, stop=stop),
        mesh=mesh,
        in_specs=placed,
        out_specs=(P("dp"), P("dp"), P("dp"), P(), P()),
        check_vma=False,
    )
```

time: 270 us -> 44.1 us (0.16)
  waiting for transfers between devices: 224 us -> 0 us
  Pallas kernels: 0 us -> 43.4 us
  other arithmetic: 14.9 us -> 0 us
  between operations: 15.5 us -> 0.64 us
  local copies, waits for them, and re-layouts: 10.2 us -> 0 us
  starting transfers between devices: 5.02 us -> 0 us
    unnamed x3 -> x0, waiting for transfers between devices: 157 us -> none
    all_gather x1 -> x0, waiting for transfers between devices: 66.8 us -> none  [on_device(): lax.all_gather(master_new.astype(jnp.bfloat16), 'dp', axis=0, tiled=True)]
    pallas_call x0 -> x2, Pallas kernels: none -> 43.4 us  [the longest x1 41.5 us: on_device(): pl.pallas_call(functools.partial(kernel, stop), out_shape=(pltpu.VMEM(sha...]
    convert_element_type x2 -> x0, other arithmetic: 10.4 us -> none  [the longest x1 8.97 us: on_device(): flat_local.astype(jnp.float32)]
    slice x7 -> x0, local copies, waits for them, and re-layouts: 7.66 us -> none  [the longest x3 3.86 us: on_device(): gate_weight = gathered[query_rows * row_width:].reshape(-1, row_width)]
    ppermute x1 -> x0, starting transfers between devices: 4.94 us -> none  [shifted(): return lax.ppermute(array, axis, pairs)]
  transfers between devices with their start and end apart: 3 -> 0, of which waited for: 2 -> 0; matrix products, arithmetic and copies ran while one was open for 5% -> 0% of each run, Pallas kernels for 0% -> 0%
where the time goes in v4:
time: 44.1 us; the launch traced here: 44 us
  Pallas kernels  43.4 us (98%)
  between operations  0.64 us (1%)
    pallas_call x1, Pallas kernels, on_device(): pl.pallas_call(functools.partial(kernel, stop), out_shape=(pltpu.VMEM(sha...  41.5 us
    pallas_call x1, Pallas kernels, on_device(): pl.pallas_call(write, out_shape=(jax.ShapeDtypeStruct((query_rows, row_wi...  1.88 us

profile of v4, /device:TPU:1, one launch (start us, length us, event | category | flops | bytes accessed | tf_op | source)
XLA Modules:
  0.0 44.0 jit_solution(6682637065289787926)
XLA Ops:
  0.6 41.5 %shard_map.101 = (f32[96,128]{1,0:T(8,128)S(1)}, f32[96,128]{1,0:T(8,128)S(1)}, f32[96,128]{1,0:T(8,128)S(1)}, bf16[4,4,4,6,32,128]{5,4,3,2,1,0:T(8,128)(2,1)S(1)}) custom-call(bf16[64,8192]{1,0:T(8,128)(2,1)} %bitcast.11, bf16[128,8192]{1,0:T(8,128)(2,1)} %bitcast.10, f32[176,128]{1,0:T(8,128)} %bitcast.12, f32[176,128]{1,0:T(8,128)} %bitcast.13, ...), custom_call_target="tpu_custom_call" | custom-call | tf_op jit(solution)/shard_map/pallas_call | solution.py:407
  42.1 1.9 %shard_map.102 = (bf16[64,8192]{1,0:T(8,128)(2,1)}, bf16[128,8192]{1,0:T(8,128)(2,1)}, f32[96,128]{1,0:T(8,128)}, f32[96,128]{1,0:T(8,128)}, f32[96,128]{1,0:T(8,128)}) custom-call(bf16[192,64,128]{2,1,0:T(8,128)(2,1)S(1)} %bitcast.9, f32[96,128]{1,0:T(8,128)S(1)} %get-tuple-element.15.new_m, f32[96,128]{1,0:T(8,128)S(1)} %get-tuple-element.16.new_v, ...), custom_call_target="tpu_custom_call" | custom-call | tf_op jit(solution)/shard_map/pallas_call | solution.py:438

commit v5 on v4

--- a/solution.py
+++ b/solution.py
@@ -23,7 +23,6 @@
 HALF = 16
 PITCH = 24
 BOUND = (48.0, 192.0)
-TURNS = (0, 1, 3, 2)
 AWAY = ((2, 2), (2, 1), (1, 2), (2, -1), (-1, 2), (1, 1), (1, -1), (-1, 1), (-1, -1),
         (2, 0), (0, 2), (1, 0), (0, 1), (-1, 0), (0, -1))
 ORDER = ((0, 1, 2), (1, 2, 0), (2, 0, 1))
@@ -76,8 +75,6 @@
             device_id=(to,), device_id_type=MESH,
         )
 
-    over = []
-
     def start(src, dst, send, recv, to):
         remote(src, dst, send_sem.at[send], recv, to).start()
 
@@ -86,16 +83,17 @@
 
     def done():
         totals = (
-            other, e0.at[:, :, pl.ds(0, 3)], e1.at[:, pl.ds(0, 15)],
-            weights.at[0, 0, pl.ds(0, 3), pl.ds(0, 3)], weights.at[0, pl.ds(0, 3), :, pl.ds(0, 3)],
-            weights.at[pl.ds(0, 3), :, :, pl.ds(0, 3)], weights.at[:, :, :, pl.ds(0, 3)],
+            other, e0.at[:, :, pl.ds(0, 3)], e1.at[:, :, pl.ds(0, 15)],
+            weights.at[0, :, :, 0, 0, pl.ds(0, 3)], weights.at[0, :, :, 0, pl.ds(0, 3)],
+            weights.at[0, :, :, pl.ds(0, 3)], weights.at[0],
         )
         for n in range({0: 1, 1: 2, 3: 3}.get(stop, 7)):
             remote(totals[n], totals[n], send_sem.at[n], s0_recv.at[0], sibling).wait_send()
-        for crosses, across in over:
-            @pl.when(crosses)
-            def _(across=across):
-                across.wait_send()
+        if stop > 1:
+            for p, on_core in ((0, 1), (2, 0)):
+                @pl.when(core == on_core)
+                def _(p=p):
+                    remote(e1.at[p, :, 0], e1.at[p, :, 0], send_sem.at[8], s0_recv.at[0], sibling).wait_send()
 
         @pl.when(hands_on)
         def _():
@@ -223,31 +221,31 @@
         round_of(3)
         return done()
 
-    for g in range(2):
+    def plane_out(g):
         for p in range(3):
             for by in (1, 3):
                 await_from(r0.at[p, g, by - 1], s1_recv.at[(p * 2 + g) * 3 + by - 1])
 
-            def gather_one(b, carry, p=p, g=g):
+            def gather_one(b, carry, p=p):
                 for c in range(4):
                     s1[p, b, c] = block(p, g, at[ORDER[p][0]], b, c) + (
                         decode(r0[p, g, 0, b, c], BOUND[0]) + decode(r0[p, g, 2, b, c], BOUND[0]))
                 return carry
 
             lax.fori_loop(0, 4, gather_one, 0)
-        if g == 1:
+        if g == 0:
             round_of(3)
         for p in range(3):
             await_from(r0.at[p, g, 1], s1_recv.at[(p * 2 + g) * 3 + 1])
 
-            def gather_two(b, carry, p=p, g=g):
+            def gather_two(b, carry, p=p):
                 for c in range(4):
                     total = s1[p, b, c] + decode(r0[p, g, 1, b, c], BOUND[0])
-                    e1[p, b * 4 + c, pl.ds(g * HALF, HALF)] = encode(total, BOUND[1])
+                    e1[p, g, b * 4 + c] = encode(total, BOUND[1])
                 return carry
 
             lax.fori_loop(0, 4, gather_two, 0)
-            if g == 0 or stop == 1:
+            if stop == 1:
                 continue
             _, b, c = ORDER[p]
             unit = 2 * p + core
@@ -256,26 +254,77 @@
             source = at[b] * 4 + at[c]
             for db, dc in AWAY:
                 start(
-                    e1.at[p, (at[b] + db) % 4 * 4 + (at[c] + dc) % 4], r1.at[place, source],
-                    2, s2_recv.at[place], device({b: db, c: dc}, owner),
+                    e1.at[p, g, (at[b] + db) % 4 * 4 + (at[c] + dc) % 4], r1.at[g, place, source],
+                    2, s2_recv.at[g * 3 + place], device({b: db, c: dc}, owner),
                 )
             if p == 1:
-                r1[place, source] = e1[p, source]
+                r1[g, place, source] = e1[p, g, source]
             else:
-                across = remote(
-                    e1.at[p, source], r1.at[place, source], send_sem.at[8], s2_recv.at[place], sibling,
-                )
                 crosses = core == (1 if p == 0 else 0)
 
                 @pl.when(crosses)
-                def _(across=across):
-                    across.start()
-
-                over.append((crosses, across))
+                def _(p=p, place=place, source=source):
+                    start(
+                        e1.at[p, g, source], r1.at[g, place, source],
+                        8, s2_recv.at[g * 3 + place], sibling,
+                    )
 
                 @pl.when(jnp.logical_not(crosses))
                 def _(p=p, place=place, source=source):
-                    r1[place, source] = e1[p, source]
+                    r1[g, place, source] = e1[p, g, source]
+
+    def group(m, g, da, db):
+        a, b, _ = ORDER[m]
+        return weights.at[core, g, m, (at[a] + da) % 4, (at[b] + db) % 4]
+
+    def step(g):
+        for m in range(3):
+            await_from(r1.at[g, m, pl.ds(0, 16 if m == 1 else 15)], s2_recv.at[g * 3 + m])
+            values = [decode(r1[g, m, n], BOUND[1]) for n in range(16)]
+            while len(values) > 1:
+                values = [one + two for one, two in zip(values[::2], values[1::2])]
+            rows = pl.ds(m * BLK + g * HALF, HALF)
+            master, moment, variance = adamw_step(new_m[rows], new_v[rows], new_s[rows], values[0])
+            new_m[rows] = master
+            new_v[rows] = moment
+            new_s[rows] = variance
+            own = weights.at[(core, g, m) + tuple(at[axis] for axis in ORDER[m])]
+            own[...] = master.astype(BF16)
+            if stop == 3:
+                continue
+            for by in (2, 1, 3):
+                start(own, own, 3, g1_recv.at[g * 3 + m], device({ORDER[m][2]: by}, core))
+
+    def group_out(m, g, db):
+        part = group(m, g, 0, -db)
+        for by in (2, 1, 3):
+            start(part, part, 5, g3_recv.at[(g * 3 + m) * 3 + by - 1], device({ORDER[m][0]: by}, core))
+
+    def second_level(g):
+        for m in range(3):
+            await_from(weights.at[0, g, m, 0, 0, pl.ds(0, 3)], g1_recv.at[g * 3 + m])
+            part = group(m, g, 0, 0)
+            for by in (2, 1, 3):
+                start(part, part, 4, g2_recv.at[(g * 3 + m) * 3 + by - 1], device({ORDER[m][1]: by}, core))
+        for m in range(3):
+            group_out(m, g, 0)
+
+    def third_level(g):
+        for by in (1, 3, 2):
+            for m in range(3):
+                await_from(group(m, g, 0, -by), g2_recv.at[(g * 3 + m) * 3 + by - 1])
+                group_out(m, g, by)
+
+    def forward(g):
+        for by in (0, 1, 3, 2):
+            for m in range(3):
+                part = weights.at[core, g, m, (at[ORDER[m][0]] - by) % 4]
+                if by:
+                    await_from(part, g3_recv.at[(g * 3 + m) * 3 + by - 1])
+                start(part, part, 6, c_recv.at[0], sibling)
+
+    for g in range(2):
+        plane_out(g)
     if stop == 1:
         return done()
 
@@ -290,68 +339,14 @@
     for n, ref in enumerate((new_m, new_v, new_s)):
         ref[...] += arrived[n]
 
-    for m in range(3):
-        await_from(r1.at[m, pl.ds(0, 16 if m == 1 else 15)], s2_recv.at[m])
-        values = [decode(r1[m, n], BOUND[1]) for n in range(16)]
-        while len(values) > 1:
-            values = [one + two for one, two in zip(values[::2], values[1::2])]
-        total = values[0]
-        rows = pl.ds(m * BLK, BLK)
-        master, moment, variance = adamw_step(new_m[rows], new_v[rows], new_s[rows], total)
-        new_m[rows] = master
-        new_v[rows] = moment
-        new_s[rows] = variance
-        weights[at[0], at[1], at[2], 3 * core + m] = master.astype(BF16)
-        if stop == 3:
-            continue
-        _, b, c = ORDER[m]
-        own = weights.at[at[0], at[1], at[2], 3 * core + m]
-        for by in (2, 1, 3):
-            start(own, own, 3, g1_recv.at[m], device({c: by}, core))
+    for g in range(2):
+        step(g)
     if stop == 3:
         return done()
-
-    def slab(m, moves, free, on_core):
-        index = [(at[axis] + moves.get(axis, 0)) % 4 for axis in range(3)]
-        for axis in free:
-            index[axis] = slice(None)
-        return weights.at[index[0], index[1], index[2], 3 * on_core + m]
-
-    def forward(m, moves, free):
-        part = slab(m, moves, free, core)
-        start(part, part, 6, c_recv.at[0], sibling)
-
-    def group_out(m, turn):
-        a, b, c = ORDER[m]
-        part = slab(m, {b: -TURNS[turn]}, (c,), core)
-        for by in (2, 1, 3):
-            start(
-                part, part, 5, g3_recv.at[m * 6 + (by - 1) * 2 + turn // 2], device({a: by}, core)
-            )
-
-    for m in range(3):
-        a, b, c = ORDER[m]
-        await_from(weights.at[0, 0, pl.ds(0, 3), m], g1_recv.at[m])
-        part = slab(m, {}, (c,), core)
-        for by in (2, 1, 3):
-            start(part, part, 4, g2_recv.at[m * 3 + by - 1], device({b: by}, core))
-        group_out(m, 0)
-    for turn in (1, 2, 3):
-        for m in range(3):
-            a, b, c = ORDER[m]
-            by = TURNS[turn]
-            await_from(slab(m, {b: -by}, (c,), core), g2_recv.at[m * 3 + by - 1])
-            group_out(m, turn)
-    for m in range(3):
-        forward(m, {}, ORDER[m][1:])
-    for part in range(2):
-        for by in (1, 3, 2):
-            for m in range(3):
-                a, b, c = ORDER[m]
-                await_from(weights.at[0, pl.ds(0, 2), :, m], g3_recv.at[m * 6 + (by - 1) * 2 + part])
-                for turn in (2 * part, 2 * part + 1):
-                    forward(m, {a: -by, b: -TURNS[turn]}, (c,))
-    await_from(weights.at[:, :, :, pl.ds(0, 3)], c_recv.at[0])
+    for stage in (second_level, third_level, forward):
+        for g in range(2):
+            stage(g)
+    await_from(weights.at[0], c_recv.at[0])
     done()
 
 
@@ -362,10 +357,18 @@
         for n, (src, dst) in enumerate(((new_m, out_m), (new_v, out_v), (new_s, out_s)))
     ]
 
-    def group(i, carry):
+    def rows_of(x, third):
+        i = 3 * x + third
         at = pl.ds(pl.multiple_of(16 * i, 16), 16)
-        for j in range(0, weights.shape[1], 8):
-            block = jnp.swapaxes(weights[at, pl.ds(j, 8)], 0, 1)
+        for j in range(0, 2 * BLK, 8):
+            picked = []
+            for row in range(16 * third, 16 * third + 16):
+                chip = (x, row // 12, row // 3 % 4)
+                unit = row % 3 * 2 + j // BLK
+                m = unit % 3
+                place = (unit // 3, j % BLK // HALF, m) + tuple(chip[axis] for axis in ORDER[m])
+                picked.append(weights[place + (pl.ds(j % HALF, 8),)])
+            block = jnp.swapaxes(jnp.stack(picked), 0, 1)
             for k in range(8):
                 tiles[at, pl.ds((j + k) * LANE, LANE)] = block[k]
 
@@ -378,11 +381,14 @@
             to = pl.ds(pl.multiple_of(16 * i - split, 16), 16)
             pltpu.make_async_copy(tiles.at[at], gate.at[to], sems.at[i]).start()
 
+    def plane(x, carry):
+        for third in range(3):
+            rows_of(x, third)
         return carry
 
     for copy in copies:
         copy.start()
-    lax.fori_loop(0, rows // 16, group, 0)
+    lax.fori_loop(0, 4, plane, 0)
     for i in range(rows // 16):
         to = query.at[pl.ds(16 * i, 16)] if 16 * i < split else gate.at[pl.ds(16 * i - split, 16)]
         copies.append(pltpu.make_async_copy(tiles.at[pl.ds(16 * i, 16)], to, sems.at[i]))
@@ -408,7 +414,7 @@
         functools.partial(kernel, stop),
         out_shape=(
             pltpu.VMEM(shard.shape, F32), pltpu.VMEM(shard.shape, F32), pltpu.VMEM(shard.shape, F32),
-            pltpu.VMEM((4, 4, 4, 6, BLK, LANE), BF16),
+            pltpu.VMEM((2, 2, 3, 4, 4, 4, HALF, LANE), BF16),
         ),
         in_specs=[hbm] * 6,
         out_specs=(vmem, vmem, vmem, vmem),
@@ -419,8 +425,8 @@
             pltpu.VMEM((3, 2, 4, 4, 4, HALF, LANE), jnp.int16),
             pltpu.VMEM((3, 2, 3, 4, 4, HALF, LANE), jnp.int16),
             pltpu.VMEM((3, 4, 4, HALF, LANE), F32),
-            pltpu.VMEM((3, 16, BLK, LANE), jnp.int16),
-            pltpu.VMEM((3, 16, BLK, LANE), jnp.int16),
+            pltpu.VMEM((3, 2, 16, HALF, LANE), jnp.int16),
+            pltpu.VMEM((2, 3, 16, HALF, LANE), jnp.int16),
             pltpu.VMEM((3, 368, LANE), F32),
             pltpu.VMEM((3, 96, LANE), F32),
             pltpu.VMEM((3, 96, LANE), F32),
@@ -428,8 +434,8 @@
             dma((4,)),
             pltpu.SemaphoreType.REGULAR((4,)),
             dma((9,)),
-            dma((2,)), dma((18,)), dma((3,)),
-            dma((3,)), dma((9,)), dma((18,)), dma((1,)), dma((1,)),
+            dma((2,)), dma((18,)), dma((6,)),
+            dma((6,)), dma((18,)), dma((18,)), dma((1,)), dma((1,)),
         ],
         compiler_params=pltpu.CompilerParams(
             collective_id=0, has_side_effects=True, vmem_limit_bytes=48 * 1024 * 1024
@@ -446,7 +452,7 @@
         out_specs=(hbm,) * 5,
         scratch_shapes=[pltpu.VMEM((rows, row_width), BF16), dma((rows // 16 + 3,))],
         compiler_params=pltpu.CompilerParams(vmem_limit_bytes=48 * 1024 * 1024),
-    )(weights.reshape(rows, row_width // LANE, LANE), new_m, new_v, new_s)
+    )(weights, new_m, new_v, new_s)
     return (new_m.reshape(-1), new_v.reshape(-1), new_s.reshape(-1), query_new, gate_new)
 
 

time: 44.1 us -> 41.5 us (0.941)
  Pallas kernels: 43.4 us -> 40.8 us
    pallas_call x1, Pallas kernels: 41.5 us -> 38.9 us  [on_device(): pl.pallas_call(functools.partial(kernel, stop), out_shape=(pltpu.VMEM(sha...]
where the time goes in v5:
time: 41.5 us; the launch traced here: 41.4 us
  Pallas kernels  40.8 us (98%)
  between operations  0.64 us (2%)
    pallas_call x1, Pallas kernels, on_device(): pl.pallas_call(functools.partial(kernel, stop), out_shape=(pltpu.VMEM(sha...  38.9 us
    pallas_call x1, Pallas kernels, on_device(): pl.pallas_call(write, out_shape=(jax.ShapeDtypeStruct((query_rows, row_wi...  1.87 us

profile of v5, /device:TPU:1, one launch (start us, length us, event | category | flops | bytes accessed | tf_op | source)
XLA Modules:
  0.0 41.4 jit_solution(689778267501738233)
XLA Ops:
  0.6 38.9 %shard_map.101 = (f32[96,128]{1,0:T(8,128)S(1)}, f32[96,128]{1,0:T(8,128)S(1)}, f32[96,128]{1,0:T(8,128)S(1)}, bf16[2,2,3,4,4,4,16,128]{7,6,5,4,3,2,1,0:T(8,128)(2,1)S(1)}) custom-call(bf16[64,8192]{1,0:T(8,128)(2,1)} %bitcast.9, bf16[128,8192]{1,0:T(8,128)(2,1)} %bitcast.8, f32[176,128]{1,0:T(8,128)} %bitcast.10, f32[176,128]{1,0:T(8,128)} %bitcast.11, ...), custom_call_target="tpu_custom_call" | custom-call | tf_op jit(solution)/shard_map/pallas_call | solution.py:413
  39.5 1.9 %shard_map.102 = (bf16[64,8192]{1,0:T(8,128)(2,1)}, bf16[128,8192]{1,0:T(8,128)(2,1)}, f32[96,128]{1,0:T(8,128)}, f32[96,128]{1,0:T(8,128)}, f32[96,128]{1,0:T(8,128)}) custom-call(bf16[2,2,3,4,4,4,16,128]{7,6,5,4,3,2,1,0:T(8,128)(2,1)S(1)} %get-tuple-element.14.weights, f32[96,128]{1,0:T(8,128)S(1)} %get-tuple-element.15.new_m, ...), custom_call_target="tpu_custom_call" | custom-call | tf_op jit(solution)/shard_map/pallas_call | solution.py:444

commit v6 on v5

--- a/solution.py
+++ b/solution.py
@@ -57,7 +57,7 @@
     query, gate, old_m, old_v, old_s, bounds_hbm,
     new_m, new_v, new_s, weights,
     mine, other, s0, e0, r0, s1, e1, r1, state, passed, arrived, bounds,
-    load_sem, near_sem, send_sem, s0_recv, s1_recv, s2_recv, g1_recv, g2_recv, g3_recv, c_recv, p_recv,
+    load_sem, near_sem, send_sem, s0_recv, s1_recv, s2_recv, g1_recv, g3_recv, c_recv, p_recv,
 ):
     me = lax.axis_index("dp")
     core = me % 2
@@ -103,6 +103,15 @@
             @pl.when(takes)
             def _():
                 handed.wait_recv()
+
+    barrier = pltpu.get_barrier_semaphore()
+    around = [sibling] + [device({axis: by}, core) for axis in range(3) for by in (1, 3)]
+
+    def greet(sem):
+        for to in around:
+            pl.semaphore_signal(sem, inc=1, device_id=(to,), device_id_type=MESH)
+
+    greet(barrier)
 
     wide = mine.shape[2]
     split = query.shape[0]
@@ -120,17 +129,21 @@
             pltpu.make_async_copy(old, state.at[n, pl.ds(96, 176)], load_sem.at[2])
         )
     olds.append(pltpu.make_async_copy(bounds_hbm, bounds, load_sem.at[3]))
-    for copy in olds + loads:
+    for copy in loads + olds:
         copy.start()
 
-    barrier = pltpu.get_barrier_semaphore()
-    around = [sibling] + [device({axis: by}, core) for axis in range(3) for by in (1, 3)]
-
-    def greet(sem):
-        for to in around:
-            pl.semaphore_signal(sem, inc=1, device_id=(to,), device_id_type=MESH)
-
-    greet(barrier)
+    pl.semaphore_wait(barrier, len(around))
+
+    for copy in swaps:
+        copy.start()
+    greet(near_sem.at[0])
+
+    hands_on = (core == 0) | (at[2] % 2 == 0)
+    takes = (core == 1) | (at[2] % 2 == 1)
+    handed = remote(
+        passed, arrived, send_sem.at[7], p_recv.at[0],
+        sibling * (1 - core) + device({2: 1}, 0) * core,
+    )
 
     for n in range(3):
         state[n, pl.ds(0, 96)] = jnp.zeros((96, LANE), F32)
@@ -150,19 +163,6 @@
         passed[n] = window(n, (me + 1) * 96)
     for n, ref in enumerate((new_m, new_v, new_s)):
         ref[...] = window(n, me * 96)
-
-    pl.semaphore_wait(barrier, len(around))
-
-    for copy in swaps:
-        copy.start()
-    greet(near_sem.at[0])
-
-    hands_on = (core == 0) | (at[2] % 2 == 0)
-    takes = (core == 1) | (at[2] % 2 == 1)
-    handed = remote(
-        passed, arrived, send_sem.at[7], p_recv.at[0],
-        sibling * (1 - core) + device({2: 1}, 0) * core,
-    )
 
     def round_of(n):
         pl.semaphore_wait(near_sem.at[n], len(around))
@@ -292,27 +292,26 @@
             own[...] = master.astype(BF16)
             if stop == 3:
                 continue
-            for by in (2, 1, 3):
-                start(own, own, 3, g1_recv.at[g * 3 + m], device({ORDER[m][2]: by}, core))
+            for db, dc in AWAY:
+                start(
+                    own, own, 4 if db else 3, g1_recv.at[(g * 3 + m) * 4 + db % 4],
+                    device({ORDER[m][1]: db, ORDER[m][2]: dc}, core),
+                )
 
     def group_out(m, g, db):
         part = group(m, g, 0, -db)
         for by in (2, 1, 3):
             start(part, part, 5, g3_recv.at[(g * 3 + m) * 3 + by - 1], device({ORDER[m][0]: by}, core))
 
-    def second_level(g):
+    def near_group(g):
         for m in range(3):
-            await_from(weights.at[0, g, m, 0, 0, pl.ds(0, 3)], g1_recv.at[g * 3 + m])
-            part = group(m, g, 0, 0)
-            for by in (2, 1, 3):
-                start(part, part, 4, g2_recv.at[(g * 3 + m) * 3 + by - 1], device({ORDER[m][1]: by}, core))
-        for m in range(3):
+            await_from(weights.at[0, g, m, 0, 0, pl.ds(0, 3)], g1_recv.at[(g * 3 + m) * 4])
             group_out(m, g, 0)
 
-    def third_level(g):
+    def other_groups(g):
         for by in (1, 3, 2):
             for m in range(3):
-                await_from(group(m, g, 0, -by), g2_recv.at[(g * 3 + m) * 3 + by - 1])
+                await_from(group(m, g, 0, -by), g1_recv.at[(g * 3 + m) * 4 + by])
                 group_out(m, g, by)
 
     def forward(g):
@@ -339,13 +338,16 @@
     for n, ref in enumerate((new_m, new_v, new_s)):
         ref[...] += arrived[n]
 
-    for g in range(2):
-        step(g)
+    step(0)
+    step(1)
     if stop == 3:
         return done()
-    for stage in (second_level, third_level, forward):
-        for g in range(2):
-            stage(g)
+    near_group(0)
+    other_groups(0)
+    near_group(1)
+    other_groups(1)
+    forward(0)
+    forward(1)
     await_from(weights.at[0], c_recv.at[0])
     done()
 
@@ -435,7 +437,7 @@
             pltpu.SemaphoreType.REGULAR((4,)),
             dma((9,)),
             dma((2,)), dma((18,)), dma((6,)),
-            dma((6,)), dma((18,)), dma((18,)), dma((1,)), dma((1,)),
+            dma((24,)), dma((18,)), dma((1,)), dma((1,)),
         ],
         compiler_params=pltpu.CompilerParams(
             collective_id=0, has_side_effects=True, vmem_limit_bytes=48 * 1024 * 1024

time: 41.5 us -> 39.8 us (0.959)
  Pallas kernels: 40.8 us -> 39.1 us
    pallas_call x1, Pallas kernels: 38.9 us -> 37.2 us  [on_device(): pl.pallas_call(functools.partial(kernel, stop), out_shape=(pltpu.VMEM(sha...]
where the time goes in v6:
time: 39.8 us; the launch traced here: 39.7 us
  Pallas kernels  39.1 us (98%)
  between operations  0.64 us (2%)
    pallas_call x1, Pallas kernels, on_device(): pl.pallas_call(functools.partial(kernel, stop), out_shape=(pltpu.VMEM(sha...  37.2 us
    pallas_call x1, Pallas kernels, on_device(): pl.pallas_call(write, out_shape=(jax.ShapeDtypeStruct((query_rows, row_wi...  1.87 us

profile of v6, /device:TPU:1, one launch (start us, length us, event | category | flops | bytes accessed | tf_op | source)
XLA Modules:
  0.0 39.7 jit_solution(13010217729256535573)
XLA Ops:
  0.6 37.2 %shard_map.101 = (f32[96,128]{1,0:T(8,128)S(1)}, f32[96,128]{1,0:T(8,128)S(1)}, f32[96,128]{1,0:T(8,128)S(1)}, bf16[2,2,3,4,4,4,16,128]{7,6,5,4,3,2,1,0:T(8,128)(2,1)S(1)}) custom-call(bf16[64,8192]{1,0:T(8,128)(2,1)} %bitcast.9, bf16[128,8192]{1,0:T(8,128)(2,1)} %bitcast.8, f32[176,128]{1,0:T(8,128)} %bitcast.10, f32[176,128]{1,0:T(8,128)} %bitcast.11, ...), custom_call_target="tpu_custom_call" | custom-call | tf_op jit(solution)/shard_map/pallas_call | solution.py:415
  37.8 1.9 %shard_map.102 = (bf16[64,8192]{1,0:T(8,128)(2,1)}, bf16[128,8192]{1,0:T(8,128)(2,1)}, f32[96,128]{1,0:T(8,128)}, f32[96,128]{1,0:T(8,128)}, f32[96,128]{1,0:T(8,128)}) custom-call(bf16[2,2,3,4,4,4,16,128]{7,6,5,4,3,2,1,0:T(8,128)(2,1)S(1)} %get-tuple-element.14.weights, f32[96,128]{1,0:T(8,128)S(1)} %get-tuple-element.15.new_m, ...), custom_call_target="tpu_custom_call" | custom-call | tf_op jit(solution)/shard_map/pallas_call | solution.py:446

commit v7 on v6

--- a/solution.py
+++ b/solution.py
@@ -187,9 +187,9 @@
                 e0[p, g, a, b, c] = encode(block(p, g, a, b, c), BOUND[0])
             return carry
 
-        lax.fori_loop(0, 4, code, 0)
+        lax.fori_loop(0, 4, code, 0, unroll=2)
         start(
-            e0.at[p, g, a], r0.at[p, g, by - 1], 1, s1_recv.at[(p * 2 + g) * 3 + by - 1],
+            e0.at[p, g, a], r0.at[p, g, by - 1], 1, s1_recv.at[(p * 2 + g) * 2 + int(by == 2)],
             device({ORDER[p][0]: by}, core),
         )
 
@@ -223,8 +223,7 @@
 
     def plane_out(g):
         for p in range(3):
-            for by in (1, 3):
-                await_from(r0.at[p, g, by - 1], s1_recv.at[(p * 2 + g) * 3 + by - 1])
+            await_from(r0.at[p, g, pl.ds(0, 2)], s1_recv.at[(p * 2 + g) * 2])
 
             def gather_one(b, carry, p=p):
                 for c in range(4):
@@ -232,11 +231,11 @@
                         decode(r0[p, g, 0, b, c], BOUND[0]) + decode(r0[p, g, 2, b, c], BOUND[0]))
                 return carry
 
-            lax.fori_loop(0, 4, gather_one, 0)
+            lax.fori_loop(0, 4, gather_one, 0, unroll=2)
         if g == 0:
             round_of(3)
         for p in range(3):
-            await_from(r0.at[p, g, 1], s1_recv.at[(p * 2 + g) * 3 + 1])
+            await_from(r0.at[p, g, 1], s1_recv.at[(p * 2 + g) * 2 + 1])
 
             def gather_two(b, carry, p=p):
                 for c in range(4):
@@ -244,7 +243,7 @@
                     e1[p, g, b * 4 + c] = encode(total, BOUND[1])
                 return carry
 
-            lax.fori_loop(0, 4, gather_two, 0)
+            lax.fori_loop(0, 4, gather_two, 0, unroll=2)
             if stop == 1:
                 continue
             _, b, c = ORDER[p]
@@ -300,7 +299,7 @@
 
     def group_out(m, g, db):
         part = group(m, g, 0, -db)
-        for by in (2, 1, 3):
+        for by in (1, 3, 2):
             start(part, part, 5, g3_recv.at[(g * 3 + m) * 3 + by - 1], device({ORDER[m][0]: by}, core))
 
     def near_group(g):
@@ -309,8 +308,8 @@
             group_out(m, g, 0)
 
     def other_groups(g):
-        for by in (1, 3, 2):
-            for m in range(3):
+        for m in range(3):
+            for by in (1, 3, 2):
                 await_from(group(m, g, 0, -by), g1_recv.at[(g * 3 + m) * 4 + by])
                 group_out(m, g, by)
 
@@ -436,7 +435,7 @@
             dma((4,)),
             pltpu.SemaphoreType.REGULAR((4,)),
             dma((9,)),
-            dma((2,)), dma((18,)), dma((6,)),
+            dma((2,)), dma((12,)), dma((6,)),
             dma((24,)), dma((18,)), dma((1,)), dma((1,)),
         ],
         compiler_params=pltpu.CompilerParams(

time: 39.8 us -> 39.6 us (level)
  no operation moved by 1% of the time
where the time goes in v7:
time: 39.6 us; the launch traced here: 39.5 us
  Pallas kernels  38.8 us (98%)
  between operations  0.64 us (2%)
    pallas_call x1, Pallas kernels, on_device(): pl.pallas_call(functools.partial(kernel, stop), out_shape=(pltpu.VMEM(sha...  37 us
    pallas_call x1, Pallas kernels, on_device(): pl.pallas_call(write, out_shape=(jax.ShapeDtypeStruct((query_rows, row_wi...  1.87 us

profile of v7, /device:TPU:1, one launch (start us, length us, event | category | flops | bytes accessed | tf_op | source)
XLA Modules:
  0.0 39.5 jit_solution(15107230840138488062)
XLA Ops:
  0.6 37.0 %shard_map.101 = (f32[96,128]{1,0:T(8,128)S(1)}, f32[96,128]{1,0:T(8,128)S(1)}, f32[96,128]{1,0:T(8,128)S(1)}, bf16[2,2,3,4,4,4,16,128]{7,6,5,4,3,2,1,0:T(8,128)(2,1)S(1)}) custom-call(bf16[64,8192]{1,0:T(8,128)(2,1)} %bitcast.9, bf16[128,8192]{1,0:T(8,128)(2,1)} %bitcast.8, f32[176,128]{1,0:T(8,128)} %bitcast.10, f32[176,128]{1,0:T(8,128)} %bitcast.11, ...), custom_call_target="tpu_custom_call" | custom-call | tf_op jit(solution)/shard_map/pallas_call | solution.py:414
  37.6 1.9 %shard_map.102 = (bf16[64,8192]{1,0:T(8,128)(2,1)}, bf16[128,8192]{1,0:T(8,128)(2,1)}, f32[96,128]{1,0:T(8,128)}, f32[96,128]{1,0:T(8,128)}, f32[96,128]{1,0:T(8,128)}) custom-call(bf16[2,2,3,4,4,4,16,128]{7,6,5,4,3,2,1,0:T(8,128)(2,1)S(1)} %get-tuple-element.14.weights, f32[96,128]{1,0:T(8,128)S(1)} %get-tuple-element.15.new_m, ...), custom_call_target="tpu_custom_call" | custom-call | tf_op jit(solution)/shard_map/pallas_call | solution.py:445
